TPU v7x, 256 devices: a whole 4x4x8 slice. The times are simulated.
256 devices in a mesh: gx: 4 (over x), gy: 8 (over y, core), gz: 8 (over z).
Axes of the slice: x: 4, y: 4, z: 8, core: 2. Of those that a mesh axis runs over, the one named last changes fastest.
Arguments:
- points: float32 [4, 8, 8, 3, 512], P('gx', 'gy', 'gz'), may hold values from -0.5 to 0.5, as said below
- band_index: int32 [4, 8, 8, 6, 64], P('gx', 'gy', 'gz'), may hold values from 0 to 512, as said below
- source: float32 [4, 8, 8, 512], P('gx', 'gy', 'gz'), may hold values from -8 to 8
- fine_first: float32 [4, 8, 8, 4, 64], P('gx', 'gy', 'gz'), may hold values from -4 to 4
- fine_mid: float32 [4, 8, 8, 2, 64, 64], P('gx', 'gy', 'gz'), may hold values from -0.75 to 0.75
- fine_last: float32 [4, 8, 8, 3, 64], P('gx', 'gy', 'gz'), may hold values from -1.5 to 1.5
- column_first: float32 [4, 8, 4, 64], P('gx', 'gy'), may hold values from -4 to 4
- column_mid: float32 [4, 8, 2, 64, 64], P('gx', 'gy'), may hold values from -0.75 to 0.75
- column_last: float32 [4, 8, 3, 64], P('gx', 'gy'), may hold values from -1.5 to 1.5
- global_first: float32 [4, 64], replicated, may hold values from -4 to 4
- global_mid: float32 [2, 64, 64], replicated, may hold values from -0.75 to 0.75
- global_last: float32 [3, 64], replicated, may hold values from -1.5 to 1.5
Outputs:
- residual: float32 [4, 8, 8, 512], P('gx', 'gy', 'gz')
- fine_first_grad: float32 [4, 8, 8, 4, 64], P('gx', 'gy', 'gz')
- fine_mid_grad: float32 [4, 8, 8, 2, 64, 64], P('gx', 'gy', 'gz')
- fine_last_grad: float32 [4, 8, 8, 3, 64], P('gx', 'gy', 'gz')
- column_first_grad: float32 [4, 8, 4, 64], P('gx', 'gy')
- column_mid_grad: float32 [4, 8, 2, 64, 64], P('gx', 'gy')
- column_last_grad: float32 [4, 8, 3, 64], P('gx', 'gy')
- global_first_grad: float32 [4, 64], replicated
- global_mid_grad: float32 [2, 64, 64], replicated
- global_last_grad: float32 [3, 64], replicated
- loss: float32 [], replicated
Inputs may be any that keep to these rules, and one draw needn't show every extreme that they name: Each point lies inside its cell. A point is within 1/8 of at most one face of its cell, and exactly the points named in band_index are within 1/8 of a face. `band_index`: row f of a subdomain lists distinct points within 1/8 of face f (faces: lower and upper along x, then y, then z), then padding entries equal to 512. The lists of one subdomain are disjoint. Each list holds 32 to 64 points, and in every subdomain some list is full.
All inputs are finite; a program needn't handle non-finite values.
Results may differ from a plain program's by a relative error of at most 0.0003.
Values sent between devices are 32-bit elements; how exact they have to be, the bound alone decides.
A program may use at most 128 MiB of HBM per device.

v0:
```python
import functools

import jax
import jax.numpy as jnp
from jax import lax
from jax.experimental import pallas as pl
from jax.experimental.pallas import tpu as pltpu
from jax.sharding import PartitionSpec as P

MESH = pl.DeviceIdType.MESH
AXES = ("gx", "gy", "gz")
f32, bf16 = jnp.float32, jnp.bfloat16
wave_square = 4.0
inverse_depth = 8.0
NT = (((1,), (1,)), ((), ()))


def split(value):
    high = value.astype(bf16)
    return high, (value - high.astype(f32)).astype(bf16)


def three(value):
    first = value.astype(bf16)
    rest = value - first.astype(f32)
    second = rest.astype(bf16)
    return first, second, (rest - second.astype(f32)).astype(bf16)


def left(matrix):
    high = matrix.astype(bf16).astype(f32)
    return jnp.concatenate([high, high, matrix - high], 1).astype(bf16)


def right(high, low):
    return jnp.concatenate([high, low, high], 0)


def dot(a, b):
    return jnp.dot(a, b, preferred_element_type=f32)


def dot_nt(a, b):
    return lax.dot_general(a, b, NT, preferred_element_type=f32)


def window(depth, facing):
    square = depth * depth
    smooth = depth * (15.0 - 10.0 * square + 3.0 * square * square) / 8.0
    blend = 0.5 * (1.0 - smooth)
    slope = (0.5 * inverse_depth * 15.0 / 8.0) * facing * (1.0 - square) * (1.0 - square)
    bend = (0.5 * inverse_depth * inverse_depth * 7.5) * depth * (1.0 - square)
    return blend, slope, bend


def kernel(
    sizes,
    chunk,
    points,
    band,
    source,
    fine_first,
    fine_mid,
    fine_last,
    column_first,
    column_mid,
    column_last,
    global_first,
    global_mid,
    global_last,
    residual_out,
    fine_first_out,
    fine_mid_out,
    fine_last_out,
    column_first_out,
    column_mid_out,
    column_last_out,
    global_first_out,
    global_mid_out,
    global_last_out,
    loss_out,
    nets,
    grads,
    f1,
    f2,
    b2,
    b1h,
    b1s,
    b1p,
    cols,
    xp,
    xpb,
    alpha,
    x0,
    x1,
    h0s,
    a1,
    a2,
    res,
    xf,
    xfb,
    falpha,
    fx0,
    fx1,
    fh0s,
    fa1,
    fa2,
    fdelta,
    hot,
    back,
    gchunks,
    cchunks,
    grs,
    gys,
    gxs,
    gag,
    crs,
    cag,
    halo_send,
    halo_recv,
    back_send,
    back_recv,
    grs_send,
    grs_recv,
    gy_send,
    gy_recv,
    gx_send,
    gx_recv,
    gag_send,
    gag_recv,
    crs_send,
    crs_recv,
    cag_send,
    cag_recv,
):
    me = tuple(lax.axis_index(axis) for axis in AXES)
    count = points.shape[1]
    slots = band.shape[1]
    pair = 2 * slots

    def peer(axis, offset):
        other = list(me)
        other[axis] = lax.rem(me[axis] + (offset + sizes[axis]), sizes[axis])
        return tuple(other)

    barrier = pltpu.get_barrier_semaphore()
    greeted = 0
    for axis in range(3):
        for offset in range(1, sizes[axis]):
            pl.semaphore_signal(barrier, inc=1, device_id=peer(axis, offset), device_id_type=MESH)
            greeted += 1

    def pack(net, first, mid, last):
        nets[net, 0:64, :] = jnp.concatenate([mid[0], mid[1]], 1)
        nets[net, 64:68, 0:64] = first[...]
        nets[net, 68:71, 0:64] = last[...]
        nets[net, 71:72, 0:64] = jnp.zeros((1, 64), f32)
        nets[net, 64:72, 64:128] = jnp.zeros((8, 64), f32)

    pack(2, fine_first, fine_mid, fine_last)
    pl.semaphore_wait(barrier, greeted)

    def halo(face):
        axis, up = face // 2, face % 2
        return pltpu.make_async_remote_copy(
            src_ref=nets.at[2],
            dst_ref=nets.at[3 + (face ^ 1)],
            send_sem=halo_send.at[face],
            recv_sem=halo_recv.at[face ^ 1],
            device_id=peer(axis, 2 * up - 1),
            device_id_type=MESH,
        )

    for face in range(6):
        halo(face).start()

    pack(1, column_first, column_mid, column_last)
    pack(0, global_first, global_mid, global_last)

    place = [me[axis].astype(f32) for axis in range(3)]

    def affine(net):
        if isinstance(net, int) and net >= 3:
            face = net - 3
            shift = [0.0, 0.0, 0.0]
            shift[face // 2] = -2.0 * (2 * (face % 2) - 1)
            return [2.0, 2.0, 2.0], shift
        scale, shift = [], []
        for axis in range(3):
            fitted_scale = 2.0 / sizes[axis]
            fitted_shift = (2.0 * place[axis] + 1.0) * (1.0 / sizes[axis]) - 1.0
            fitted = (net == 0) if axis < 2 else (net <= 1)
            scale.append(jnp.where(fitted, fitted_scale, 2.0))
            shift.append(jnp.where(fitted, fitted_shift, 0.0))
        return scale, shift

    def prepare(net, scale, shift):
        mats = nets[net, 0:64, :]
        turned = mats.T
        rows = nets[net, 64:72, :]
        turned_rows = rows.T
        m1 = mats[:, 0:64]
        m1t = turned[0:64]
        row = [scale[d] * rows[d : d + 1, 0:64] for d in range(3)]
        col = [scale[d] * turned_rows[0:64, d : d + 1] for d in range(3)]
        square_row = -2.0 * (row[0] * row[0] + row[1] * row[1] + row[2] * row[2])
        square_col = -2.0 * (col[0] * col[0] + col[1] * col[1] + col[2] * col[2])
        bias = turned_rows[0:64, 3:4]
        for d in range(3):
            bias = bias + shift[d] * turned_rows[0:64, d : d + 1]
        f1[net, 0:64, :] = left(m1)
        b1h[net] = left(m1t)
        for d in range(3):
            f1[net, 64 * (d + 1) : 64 * (d + 2), :] = left(m1 * row[d])
            b1s[net, :, 192 * d : 192 * (d + 1)] = left(m1t * col[d])
        f1[net, 256:320, :] = left(m1 * square_row)
        b1p[net] = left(m1t * square_col)
        f2[net] = left(mats[:, 64:128])
        b2[net] = left(turned[64:128])
        lane = lax.broadcasted_iota(jnp.int32, (64, 8), 1)
        kept = turned_rows[0:64, 0:8]
        for d in range(3):
            kept = jnp.where(lane == d, col[d], kept)
        cols[net, :, 0:8] = jnp.where(lane == 3, bias, kept)

    xyz = points[...]
    lane_ones = jnp.ones((1, count), f32)
    xp[0:3, :] = xyz
    xp[3:4, :] = lane_ones
    xp[4:8, :] = jnp.zeros((4, count), f32)
    x_terms = three(xp[...])
    xpb[...] = jnp.zeros(xpb.shape, bf16)
    xpb[0:16, :] = jnp.concatenate([x_terms[0].astype(f32), x_terms[1].astype(f32)], 0).astype(bf16)

    def present(axis, facing):
        if facing < 0:
            return jnp.where(me[axis] > 0, 1.0, 0.0).astype(f32)
        return jnp.where(me[axis] < sizes[axis] - 1, 1.0, 0.0).astype(f32)

    inside = lane_ones
    curve = jnp.zeros((1, count), f32)
    for axis in range(3):
        along = xyz[axis : axis + 1]
        upper = along > 0.0
        facing = jnp.where(upper, 1.0, -1.0)
        depth = jnp.minimum((0.5 - jnp.abs(along)) * inverse_depth, 1.0)
        exists = jnp.where(upper, present(axis, 1), present(axis, -1))
        blend, slope, bend = window(depth, facing)
        inside = inside - exists * blend
        curve = curve - exists * bend
        alpha[2, 1 + axis : 2 + axis, :] = -2.0 * exists * slope
    alpha[2, 0:1, :] = wave_square * inside + curve
    alpha[2, 4:5, :] = inside
    for net in (0, 1):
        alpha[net, 0:1, :] = wave_square * lane_ones
        alpha[net, 1:4, :] = jnp.zeros((3, count), f32)
        alpha[net, 4:5, :] = lane_ones

    half = lax.broadcasted_iota(jnp.int32, (1, pair), 1) < slots
    point_id = lax.broadcasted_iota(jnp.int32, (count, pair), 0)
    stacked = jnp.concatenate([term.astype(f32) for term in x_terms], 0).astype(bf16)
    for axis in range(3):
        listed = jnp.concatenate([band[2 * axis : 2 * axis + 1, :], band[2 * axis + 1 : 2 * axis + 2, :]], 1)
        hot[axis] = jnp.where(point_id == listed, 1.0, 0.0).astype(bf16)
        taken = dot(stacked, hot[axis])
        taken = taken[0:8] + taken[8:16] + taken[16:24]
        xf[axis] = taken
        high, low = split(taken)
        xfb[axis] = jnp.zeros(xfb.shape[1:], bf16)
        xfb[axis, 0:16, :] = jnp.concatenate([high.astype(f32), low.astype(f32)], 0).astype(bf16)
        facing = jnp.where(half, -1.0, 1.0)
        exists = jnp.where(half, present(axis, -1), present(axis, 1))
        depth = jnp.minimum((0.5 - facing * taken[axis : axis + 1]) * inverse_depth, 1.0)
        blend, slope, bend = window(depth, facing)
        falpha[axis, 0:1, :] = exists * (wave_square * blend + bend)
        falpha[axis, 1:4, :] = jnp.zeros((3, pair), f32)
        falpha[axis, 1 + axis : 2 + axis, :] = 2.0 * exists * slope
        falpha[axis, 4:5, :] = exists * blend

    def tanh_layer(z, f, m):
        h = jnp.tanh(z)
        s = 1.0 - h * h
        q = f[0] * f[0] + f[1] * f[1] + f[2] * f[2]
        return h, s, q, m - 2.0 * h * q

    def forward(get, x, al, mm, keep0, keep1, keep2):
        z = get(0) * x[0:1] + get(1) * x[1:2] + get(2) * x[2:3] + get(3)
        h = jnp.tanh(z)
        s = 1.0 - h * h
        p = h * s
        parts = [split(v) for v in (h, s, p)]
        keep0(h, parts)
        m1h = mm(f1, 0, 64, right(*parts[0]))
        m1f = mm(f1, 64, 256, right(*parts[1]))
        m1l = mm(f1, 256, 320, right(*parts[2]))
        f = [m1f[64 * d : 64 * (d + 1)] for d in range(3)]
        h, s, q, w = tanh_layer(m1h + get(4), f, m1l)
        parts = [split(v) for v in (h, s * f[0], s * f[1], s * f[2], s * w)]
        keep1(h, f, q, w, parts)
        n = x.shape[1]
        out = mm(f2, 0, 64, jnp.concatenate([right(*part) for part in parts], 1))
        out = [out[:, n * k : n * (k + 1)] for k in range(5)]
        f = out[1:4]
        h, s, q, w = tanh_layer(out[0] + get(5), f, out[4])
        u = al[1:2] * f[0] + al[2:3] * f[1] + al[3:4] * f[2] + al[4:5] * w
        c = al[0:1] * h + s * u
        keep2(h, f, q, u, c)
        return jnp.sum(get(6) * c, axis=0, keepdims=True)

    def backward(get, al, delta, mm, lane_sum, saved0, saved1, saved2):
        h, fa, fb, fc, q, u, c = saved2
        f = (fa, fb, fc)
        dlast = lane_sum(delta * c)
        e = get(6) * delta
        s = 1.0 - h * h
        es = e * s
        gm = es * al[4:5]
        k = 4.0 * h * gm
        gf = [es * al[1 + d : 2 + d] - k * f[d] for d in range(3)]
        gz = (e * al[0:1] - 2.0 * (q * gm + h * (e * u))) * s
        dbias1 = lane_sum(gz)
        g2 = [split(v) for v in (gz, gf[0], gf[1], gf[2], gm)]
        out = mm(b2, 0, 64, jnp.concatenate([right(*part) for part in g2], 1))
        n = e.shape[1]
        oh, oa, ob, oc, ol = [out[:, n * k : n * (k + 1)] for k in range(5)]
        o = (oa, ob, oc)
        h, fa, fb, fc, q, w = saved1
        f = (fa, fb, fc)
        s = 1.0 - h * h
        gm = ol * s
        k = 4.0 * h * gm
        gf = [o[d] * s - k * f[d] for d in range(3)]
        gs = o[0] * f[0] + o[1] * f[1] + o[2] * f[2] + ol * w
        gz = (oh - 2.0 * (q * gm + h * gs)) * s
        dbias0 = lane_sum(gz)
        g1 = [split(v) for v in (gz, gf[0], gf[1], gf[2], gm)]
        oh = mm(b1h, 0, 64, right(*g1[0]))
        os = mm(b1s, 0, 64, jnp.concatenate([right(*part) for part in g1[1:4]], 0))
        op = mm(b1p, 0, 64, right(*g1[4]))
        h = saved0
        s = 1.0 - h * h
        gz = (oh + op * s - 2.0 * h * (os + op * h)) * s
        return g2, g1, split(gz), dlast, dbias1, dbias0

    def fold(product):
        return product[0:64] + product[64:128]

    def finish(net, scale, shift, dm2, ah, af, al, pts, dlast, dbias1, dbias0, extra):
        lane = lax.broadcasted_iota(jnp.int32, (64, 128), 1)
        pts = jnp.where(lane == 4, dbias0, pts)
        pts = jnp.where(lane == 5, dbias1, pts)
        pts = jnp.where(lane == 6, dlast, pts)
        turned = pts.T
        sums = turned[0:8] + turned[8:16]
        m1 = nets[net, 0:64, 0:64]
        rows = nets[net, 64:72, 0:64]
        row = [scale[d] * rows[d : d + 1] for d in range(3)]
        square = row[0] * row[0] + row[1] * row[1] + row[2] * row[2]
        dsquare = -2.0 * jnp.sum(m1 * al, axis=0, keepdims=True)
        dm1 = ah - 2.0 * (al * square)
        first = []
        for d in range(3):
            dm1 = dm1 + af[d] * row[d]
            slope = sums[d : d + 1] + jnp.sum(m1 * af[d], axis=0, keepdims=True) + 2.0 * row[d] * dsquare
            first.append(scale[d] * slope + shift[d] * sums[3:4])
        grads[net, 0:64, :] = jnp.concatenate([dm1, dm2], 1)
        grads[net, 64:72, 0:64] = jnp.concatenate(first + [sums[3:7], extra], 0)
        grads[net, 64:72, 64:128] = jnp.zeros((8, 64), f32)

    def row_sums(value):
        return jnp.sum(value, axis=1, keepdims=True)

    def half_sums(value):
        return row_sums(jnp.where(half, value, 0.0)), row_sums(jnp.where(half, 0.0, value))

    def forward_wide(net):
        def get(k):
            return cols[net, :, k : k + 1]

        def mm(ref, low, high, rhs):
            return dot(ref[net, low:high, :], rhs)

        for start in range(0, count, chunk):
            span = slice(start, start + chunk)

            def keep0(h, parts):
                h0s[net, :, span] = h
                for k, part in enumerate(parts):
                    x0[net, k, 0:64, span] = part[0]
                    x0[net, k, 64:128, span] = part[1]

            def keep1(h, f, q, w, parts):
                for k, value in enumerate((h, f[0], f[1], f[2], q, w)):
                    a1[net, k, :, span] = value
                for k, part in enumerate(parts):
                    x1[net, k, 0:64, span] = part[0]
                    x1[net, k, 64:128, span] = part[1]

            def keep2(h, f, q, u, c):
                for k, value in enumerate((h, f[0], f[1], f[2], q, u, c)):
                    a2[net, k, :, span] = value

            row = forward(get, xp[:, span], alpha[net, :, span], mm, keep0, keep1, keep2)
            res[0:1, span] = res[0:1, span] + row

    def backward_wide(net, extra):
        def get(k):
            return cols[net, :, k : k + 1]

        def mm(ref, low, high, rhs):
            return dot(ref[net, low:high, :], rhs)

        g2, g1, g0, sums = [], [], [], None
        for start in range(0, count, chunk):
            span = slice(start, start + chunk)
            part = backward(
                get,
                alpha[net, :, span],
                res[1:2, span],
                mm,
                row_sums,
                h0s[net, :, span],
                [a1[net, k, :, span] for k in range(6)],
                [a2[net, k, :, span] for k in range(7)],
            )
            g2.append(part[0])
            g1.append(part[1])
            g0.append(part[2])
            sums = part[3:] if sums is None else tuple(a + b for a, b in zip(sums, part[3:]))

        def stack(pieces):
            return jnp.concatenate([jnp.concatenate(piece, 0) for piece in pieces], 1)

        lhs = jnp.concatenate([stack([g[k] for g in g2]) for k in range(5)], 1)
        rhs = jnp.concatenate([x1[net, k] for k in range(5)], 1)
        dm2 = fold(dot_nt(lhs, rhs))
        ah = fold(dot_nt(stack([g[0] for g in g1]), x0[net, 0]))
        lhs = jnp.concatenate([stack([g[1 + d] for g in g1]) for d in range(3)], 0)
        af = dot_nt(lhs, x0[net, 1])
        al = fold(dot_nt(stack([g[4] for g in g1]), x0[net, 2]))
        pts = fold(dot_nt(stack(g0), xpb[...]))
        af = [fold(af[128 * d : 128 * (d + 1)]) for d in range(3)]

        def sides(value):
            return value[:, 0:64] + value[:, 64:128]

        scale, shift = affine(net)
        finish(net, scale, shift, sides(dm2), sides(ah), [sides(v) for v in af], sides(al), pts, *sums, extra)

    wide_half = (lax.broadcasted_iota(jnp.int32, (1, 5 * pair), 1) & (pair - 1)) < slots

    def pair_tools(axis):
        net = 3 + 2 * axis

        def get(k):
            return jnp.where(half, cols[net, :, k : k + 1], cols[net + 1, :, k : k + 1])

        def mm(ref, low, high, rhs):
            rows = high - low
            lhs = jnp.concatenate([ref[net, low:high, :], ref[net + 1, low:high, :]], 0)
            out = dot(lhs, rhs)
            return jnp.where(wide_half[:, 0 : rhs.shape[1]], out[0:rows], out[rows : 2 * rows])

        return net, get, mm

    first_half = jnp.where(half, 1.0, 0.0).astype(bf16)
    second_half = jnp.where(half, 0.0, 1.0).astype(bf16)

    def forward_pair(axis):
        net, get, mm = pair_tools(axis)

        def keep_parts(ref, parts):
            for k, part in enumerate(parts):
                ref[axis, k, 0:64, :] = part[0] * first_half
                ref[axis, k, 64:128, :] = part[1] * first_half
                ref[axis, k, 128:192, :] = part[0] * second_half
                ref[axis, k, 192:256, :] = part[1] * second_half

        def keep0(h, parts):
            fh0s[axis] = h
            keep_parts(fx0, parts)

        def keep1(h, f, q, w, parts):
            for k, value in enumerate((h, f[0], f[1], f[2], q, w)):
                fa1[axis, k] = value
            keep_parts(fx1, parts)

        def keep2(h, f, q, u, c):
            for k, value in enumerate((h, f[0], f[1], f[2], q, u, c)):
                fa2[axis, k] = value

        row = forward(get, xf[axis], falpha[axis], mm, keep0, keep1, keep2)
        terms = jnp.concatenate([term.astype(f32) for term in three(row)] + [jnp.zeros((5, pair), f32)], 0)
        spread = dot_nt(terms.astype(bf16), hot[axis])
        res[0:1, :] = res[0:1, :] + (spread[0:1] + spread[1:2] + spread[2:3])

    def backward_pair(axis):
        net, get, mm = pair_tools(axis)
        delta = fdelta[axis, 0:1, :]
        al = falpha[axis]
        g2, g1, g0, dlast, dbias1, dbias0 = backward(
            get,
            al,
            delta,
            mm,
            half_sums,
            fh0s[axis],
            [fa1[axis, k] for k in range(6)],
            [fa2[axis, k] for k in range(7)],
        )

        def stack(piece):
            return jnp.concatenate(piece, 0)

        dm2 = fold(
            dot_nt(
                jnp.concatenate([stack(g) for g in g2], 1),
                jnp.concatenate([fx1[axis, k] for k in range(5)], 1),
            )
        )
        ah = fold(dot_nt(stack(g1[0]), fx0[axis, 0]))
        af = dot_nt(jnp.concatenate([stack(g1[1 + d]) for d in range(3)], 0), fx0[axis, 1])
        af = [fold(af[128 * d : 128 * (d + 1)]) for d in range(3)]
        al = fold(dot_nt(stack(g1[4]), fx0[axis, 2]))
        points_here = xfb[axis]
        for side in range(2):
            kept = first_half if side == 0 else second_half
            pts = fold(dot_nt(stack(g0), points_here * kept))

            def sides(value):
                return value[:, 128 * side : 128 * side + 64] + value[:, 128 * side + 64 : 128 * side + 128]

            scale = [2.0, 2.0, 2.0]
            shift = [jnp.where(axis == d, 2.0 - 4.0 * side, 0.0) for d in range(3)]
            finish(
                net + side,
                scale,
                shift,
                sides(dm2),
                sides(ah),
                [sides(v) for v in af],
                sides(al),
                pts,
                dlast[side],
                dbias1[side],
                dbias0[side],
                jnp.zeros((1, 64), f32),
            )

    def spread_out(axis, source_of, ref, send, recv):
        for offset in range(1, sizes[axis]):
            target = lax.rem(me[axis] + offset, sizes[axis])
            pltpu.make_async_remote_copy(
                src_ref=source_of(target),
                dst_ref=ref.at[me[axis]],
                send_sem=send.at[offset],
                recv_sem=recv.at[me[axis]],
                device_id=peer(axis, offset),
                device_id_type=MESH,
            ).start()

    def collect(axis, source_of, ref, send, recv):
        for offset in range(1, sizes[axis]):
            target = lax.rem(me[axis] + offset, sizes[axis])
            sender = lax.rem(me[axis] + (sizes[axis] - offset), sizes[axis])
            copy = pltpu.make_async_remote_copy(
                src_ref=source_of(target),
                dst_ref=ref.at[sender],
                send_sem=send.at[offset],
                recv_sem=recv.at[sender],
                device_id=peer(axis, offset),
                device_id_type=MESH,
            )
            copy.wait()

    def total(ref, number):
        value = ref[0]
        for k in range(1, number):
            value = value + ref[k]
        return value

    def chunked(ref, net):
        rows = 64 // sizes[2]
        for k in range(sizes[2]):
            ref[k, 0:rows, :] = grads[net, rows * k : rows * (k + 1), :]
            ref[k, rows : rows + 8 // sizes[2], :] = grads[net, 64 + 8 // sizes[2] * k : 64 + 8 // sizes[2] * (k + 1), :]

    def unchunk(ref, first_ref, mid_ref, last_ref, loss_ref):
        rows = 64 // sizes[2]
        extras = []
        for k in range(sizes[2]):
            block = ref[k]
            mid_ref[0, rows * k : rows * (k + 1), :] = block[0:rows, 0:64]
            mid_ref[1, rows * k : rows * (k + 1), :] = block[0:rows, 64:128]
            extras.append(block[rows : rows + 8 // sizes[2], 0:64])
        extras = jnp.concatenate(extras, 0)
        first_ref[...] = extras[0:4]
        last_ref[...] = extras[4:7]
        if loss_ref is not None:
            loss_ref[...] = extras[7:8, 0:1]

    g_rs = (2, lambda target: gchunks.at[target], grs, grs_send, grs_recv)
    c_rs = (2, lambda target: cchunks.at[target], crs, crs_send, crs_recv)
    g_y = (1, lambda target: gys.at[me[1]], gys, gy_send, gy_recv)
    g_x = (0, lambda target: gxs.at[me[0]], gxs, gx_send, gx_recv)
    g_ag = (2, lambda target: gag.at[me[2]], gag, gag_send, gag_recv)
    c_ag = (2, lambda target: cag.at[me[2]], cag, cag_send, cag_recv)

    def send_back(face):
        axis, up = face // 2, face % 2
        return pltpu.make_async_remote_copy(
            src_ref=grads.at[3 + face],
            dst_ref=back.at[face ^ 1],
            send_sem=back_send.at[face],
            recv_sem=back_recv.at[face ^ 1],
            device_id=peer(axis, 2 * up - 1),
            device_id_type=MESH,
        )

    res[0:1, :] = -source[...]

    def prepare_wide(net, carry):
        prepare(net, *affine(net))
        forward_wide(net)
        return carry

    lax.fori_loop(0, 3, prepare_wide, 0)
    gchunks[...] = jnp.zeros(gchunks.shape, f32)
    cchunks[...] = jnp.zeros(cchunks.shape, f32)

    for face in range(6):
        halo(face).wait()

    def face_shift(axis, side):
        return [jnp.where(axis == d, 2.0 - 4.0 * side, 0.0) for d in range(3)]

    def forward_faces(axis, carry):
        for side in range(2):
            prepare(3 + 2 * axis + side, [2.0, 2.0, 2.0], face_shift(axis, side))
        forward_pair(axis)
        return carry

    lax.fori_loop(0, 3, forward_faces, 0)

    residual = res[0:1, :]
    residual_out[...] = residual
    delta = residual * (1.0 / count)
    res[1:2, :] = delta
    loss = jnp.sum(residual * residual, axis=1, keepdims=True) * (0.5 / count)
    terms = jnp.concatenate([term.astype(f32) for term in three(delta)] + [jnp.zeros((5, count), f32)], 0)
    terms = terms.astype(bf16)
    for axis in range(3):
        taken = dot(terms, hot[axis])
        fdelta[axis, 0:1, :] = taken[0:1] + taken[1:2] + taken[2:3]

    first_lane = lax.broadcasted_iota(jnp.int32, (1, 64), 1) == 0

    def backward_two(net, carry):
        extra = jnp.where(first_lane & (net == 0), loss, 0.0)
        backward_wide(net, extra)
        return carry

    lax.fori_loop(0, 2, backward_two, 0)
    chunked(gchunks, 0)
    chunked(cchunks, 1)
    grs[me[2]] = gchunks[me[2]]
    crs[me[2]] = cchunks[me[2]]
    spread_out(*g_rs)
    spread_out(*c_rs)

    def backward_faces(axis, carry):
        backward_pair(axis)
        return carry

    lax.fori_loop(0, 3, backward_faces, 0)
    for face in range(6):
        send_back(face).start()

    collect(*g_rs)
    gys[me[1]] = total(grs, sizes[2])
    spread_out(*g_y)
    collect(*c_rs)
    cag[me[2]] = total(crs, sizes[2])
    spread_out(*c_ag)

    backward_wide(2, jnp.zeros((1, 64), f32))

    collect(*g_y)
    gxs[me[0]] = total(gys, sizes[1])
    spread_out(*g_x)
    collect(*c_ag)
    unchunk(cag, column_first_out, column_mid_out, column_last_out, None)
    for face in range(6):
        send_back(face).wait()
    collect(*g_x)
    gag[me[2]] = total(gxs, sizes[0])
    spread_out(*g_ag)
    fine = grads[2] + total(back, 6)
    fine_mid_out[0] = fine[0:64, 0:64]
    fine_mid_out[1] = fine[0:64, 64:128]
    fine_first_out[...] = fine[64:68, 0:64]
    fine_last_out[...] = fine[68:71, 0:64]
    collect(*g_ag)
    unchunk(gag, global_first_out, global_mid_out, global_last_out, loss_out)


def step(sizes, points, band_index, source, *params):
    count = points.shape[-1]
    slots = band_index.shape[-1]
    chunk = 256
    pair = 2 * slots
    shapes = [(4, 64), (2, 64, 64), (3, 64)]
    operands = [points.reshape(3, count), band_index.reshape(6, slots), source.reshape(1, count)]
    operands += [param.reshape(shapes[k % 3]) for k, param in enumerate(params)]
    outs = [(1, count)] + shapes * 3 + [(1, 1)]
    vmem = pltpu.VMEM
    block = 16 * max(1, 8 // sizes[2])
    scratch = [
        vmem((9, 72, 128), f32),
        vmem((9, 72, 128), f32),
        vmem((9, 320, 192), bf16),
        vmem((9, 64, 192), bf16),
        vmem((9, 64, 192), bf16),
        vmem((9, 64, 192), bf16),
        vmem((9, 64, 576), bf16),
        vmem((9, 64, 192), bf16),
        vmem((9, 64, 128), f32),
        vmem((8, count), f32),
        vmem((128, count), bf16),
        vmem((3, 8, count), f32),
        vmem((3, 3, 128, count), bf16),
        vmem((3, 5, 128, count), bf16),
        vmem((3, 64, count), f32),
        vmem((3, 6, 64, count), f32),
        vmem((3, 7, 64, count), f32),
        vmem((8, count), f32),
        vmem((3, 8, pair), f32),
        vmem((3, 128, pair), bf16),
        vmem((3, 8, pair), f32),
        vmem((3, 3, 256, pair), bf16),
        vmem((3, 5, 256, pair), bf16),
        vmem((3, 64, pair), f32),
        vmem((3, 6, 64, pair), f32),
        vmem((3, 7, 64, pair), f32),
        vmem((3, 8, pair), f32),
        vmem((3, count, pair), bf16),
        vmem((6, 72, 128), f32),
        vmem((sizes[2], block, 128), f32),
        vmem((sizes[2], block, 128), f32),
        vmem((sizes[2], block, 128), f32),
        vmem((sizes[1], block, 128), f32),
        vmem((sizes[0], block, 128), f32),
        vmem((sizes[2], block, 128), f32),
        vmem((sizes[2], block, 128), f32),
        vmem((sizes[2], block, 128), f32),
    ]
    dma = pltpu.SemaphoreType.DMA
    scratch += [dma((6,))] * 4
    scratch += [dma((sizes[k],)) for k in (2, 2, 1, 1, 0, 0, 2, 2, 2, 2, 2, 2)]
    whole = pl.BlockSpec(memory_space=pltpu.VMEM)
    results = pl.pallas_call(
        functools.partial(kernel, sizes, chunk),
        out_shape=[jax.ShapeDtypeStruct(shape, f32) for shape in outs],
        in_specs=[whole] * 12,
        out_specs=[whole] * 11,
        scratch_shapes=scratch,
        compiler_params=pltpu.CompilerParams(
            collective_id=0, has_side_effects=True, vmem_limit_bytes=40 << 20
        ),
        cost_estimate=pl.CostEstimate(flops=500_000_000, bytes_accessed=1_000_000, transcendentals=400_000),
        name="training_step",
    )(*operands)
    lead = [(1, 1, 1)] * 4 + [(1, 1)] * 3 + [()] * 3
    arrays = [results[0].reshape(1, 1, 1, count)]
    arrays += [value.reshape(front + value.shape) for value, front in zip(results[1:10], lead[1:])]
    return tuple(arrays) + (results[10].reshape(()),)


def solution(mesh):
    sizes = tuple(mesh.shape[axis] for axis in AXES)
    cell = ("gx", "gy", "gz")
    column = ("gx", "gy")
    in_specs = (P(*cell, None, None), P(*cell, None, None), P(*cell, None))
    nets_specs = (
        (P(*cell, None, None), P(*cell, None, None, None), P(*cell, None, None))
        + (P(*column, None, None), P(*column, None, None, None), P(*column, None, None))
        + (P(), P(), P())
    )
    return jax.shard_map(
        functools.partial(step, sizes),
        mesh=mesh,
        in_specs=in_specs + nets_specs,
        out_specs=(P(*cell, None),) + nets_specs + (P(),),
        check_vma=False,
    )
```

profile of v0, /device:TPU:1, one launch (start us, length us, event | category | flops | bytes accessed | tf_op | source)
XLA Modules:
  0.0 51.9 jit_solution(6654686275340842578)
XLA Ops:
  0.6 0.0 copy-start.10
  0.7 0.7 %copy-done.10 = f32[1,1,1,3,64]{4,2,3,1,0:T(1,128)S(1)} copy-done((f32[1,1,1,3,64]{4,2,3,1,0:T(1,128)S(1)}, f32[1,1,1,3,64]{4,2,3,1,0:T(1,128)}, u32[]{:S(2)}) %copy-start.10) | copy-done | bytes 792
  1.3 0.0 copy-start.11
  1.3 0.7 %copy-done.11 = f32[1,1,3,64]{3,1,2,0:T(1,128)S(1)} copy-done((f32[1,1,3,64]{3,1,2,0:T(1,128)S(1)}, f32[1,1,3,64]{3,1,2,0:T(1,128)}, u32[]{:S(2)}) %copy-start.11) | copy-done | bytes 792
  2.0 0.0 copy-start.9
  2.0 0.0 copy-start.8
  2.0 0.7 %copy-done.9 = s32[1,1,1,6,64]{4,2,3,1,0:T(1,128)S(1)} copy-done((s32[1,1,1,6,64]{4,2,3,1,0:T(1,128)S(1)}, s32[1,1,1,6,64]{4,2,3,1,0:T(1,128)}, u32[]{:S(2)}) %copy-start.9) | copy-done | bytes 1560
  2.7 0.0 copy-done.8
  2.7 0.0 copy-start.3
  2.7 0.0 copy-start.4
  2.7 0.0 copy-start.5
  2.7 0.0 copy-start.6
  2.7 0.0 copy-start.7
  2.8 0.6 %copy-done.3 = f32[1,1,1,512]{3,2,1,0:T(1,128)S(1)} copy-done((f32[1,1,1,512]{3,2,1,0:T(1,128)S(1)}, f32[1,1,1,512]{3,2,1,0:T(1,128)}, u32[]{:S(2)}) %copy-start.3) | copy-done | bytes 2072
  3.4 0.0 copy-done.4
  3.4 0.0 copy-done.5
  3.4 0.0 copy-done.6
  3.4 0.0 copy-done.7
  3.5 0.0 copy-start
  3.5 0.8 %copy-done = f32[1,1,1,2,64,64]{5,4,3,2,1,0:T(8,128)S(1)} copy-done((f32[1,1,1,2,64,64]{5,4,3,2,1,0:T(8,128)S(1)}, f32[1,1,1,2,64,64]{5,4,3,2,1,0:T(8,128)}, u32[]{:S(2)}) %copy-start) | copy-done | bytes 32792
  4.3 0.0 copy-start.1
  4.3 0.8 %copy-done.1 = f32[1,1,2,64,64]{4,3,2,1,0:T(8,128)S(1)} copy-done((f32[1,1,2,64,64]{4,3,2,1,0:T(8,128)S(1)}, f32[1,1,2,64,64]{4,3,2,1,0:T(8,128)}, u32[]{:S(2)}) %copy-start.1) | copy-done | bytes 32792
  5.1 0.0 copy-start.2
  5.1 0.8 %copy-done.2 = f32[2,64,64]{2,1,0:T(8,128)S(1)} copy-done((f32[2,64,64]{2,1,0:T(8,128)S(1)}, f32[2,64,64]{2,1,0:T(8,128)}, u32[]{:S(2)}) %copy-start.2) | copy-done | bytes 32792
  6.0 38.2 %training_step.1 = (f32[1,512]{1,0:T(1,128)S(1)}, f32[4,64]{1,0:T(4,128)S(1)}, f32[2,64,64]{2,1,0:T(8,128)S(1)}, f32[3,64]{1,0:T(4,128)S(1)}, f32[4,64]{1,0:T(4,...) custom-call(f32[3,512]{1,0:T(4,128)S(1)} %bitcast.27, ...), custom_call_target="tpu_custom_call" | custom-call | flops 500000000 | bytes 1000000 | tf_op jit(solution)/shard_map/training_step/pallas_call | solution.py:761
  44.2 0.6 %copy.23 = f32[1,1,1,3,64]{4,2,3,1,0:T(1,128)} copy(f32[1,1,1,3,64]{4,3,2,1,0:T(4,128)S(1)} %bitcast.30) | data formatting | bytes 1536
  44.8 0.6 %copy.24 = f32[1,1,3,64]{3,1,2,0:T(1,128)} copy(f32[1,1,3,64]{3,2,1,0:T(4,128)S(1)} %bitcast.29) | data formatting | bytes 1536
  45.4 0.6 %copy.46 = f32[1,1,1,512]{3,2,1,0:T(1,128)} copy(f32[1,1,1,512]{3,2,1,0:T(1,128)S(1)} %bitcast.35) | data formatting | bytes 4096
  45.9 0.6 %copy.47 = f32[1,1,1,4,64]{4,3,2,1,0:T(4,128)} copy(f32[1,1,1,4,64]{4,3,2,1,0:T(4,128)S(1)} %bitcast.34) | data formatting | bytes 2048
  46.5 0.6 %copy.48 = f32[1,1,1,2,64,64]{5,4,3,2,1,0:T(8,128)} copy(f32[1,1,1,2,64,64]{5,4,3,2,1,0:T(8,128)S(1)} %bitcast.26) | data formatting | bytes 65536
  47.1 0.6 %copy.49 = f32[1,1,4,64]{3,2,1,0:T(4,128)} copy(f32[1,1,4,64]{3,2,1,0:T(4,128)S(1)} %bitcast.33) | data formatting | bytes 2048
  47.7 0.6 %copy.50 = f32[1,1,2,64,64]{4,3,2,1,0:T(8,128)} copy(f32[1,1,2,64,64]{4,3,2,1,0:T(8,128)S(1)} %bitcast.25) | data formatting | bytes 65536
  48.4 0.6 %copy.51 = f32[4,64]{1,0:T(4,128)} copy(f32[4,64]{1,0:T(4,128)S(1)} %get-tuple-element.62) | data formatting | bytes 2048
  48.9 0.6 %copy.52 = f32[2,64,64]{2,1,0:T(8,128)} copy(f32[2,64,64]{2,1,0:T(8,128)S(1)} %get-tuple-element.63) | data formatting | bytes 65536
  49.6 0.6 %copy.53 = f32[3,64]{1,0:T(4,128)} copy(f32[3,64]{1,0:T(4,128)S(1)} %get-tuple-element.64) | data formatting | bytes 1536
  (4 shorter events, 0.0 us)
Async XLA Ops:
  0.6 0.7 %copy-start.10 = (f32[1,1,1,3,64]{4,2,3,1,0:T(1,128)S(1)}, f32[1,1,1,3,64]{4,2,3,1,0:T(1,128)}, u32[]{:S(2)}) copy-start(f32[1,1,1,3,64]{4,2,3,1,0:T(1,128)} %param.17) | copy-start | bytes 2308
  1.3 0.7 %copy-start.11 = (f32[1,1,3,64]{3,1,2,0:T(1,128)S(1)}, f32[1,1,3,64]{3,1,2,0:T(1,128)}, u32[]{:S(2)}) copy-start(f32[1,1,3,64]{3,1,2,0:T(1,128)} %param.20) | copy-start | bytes 2308
  2.0 0.7 %copy-start.9 = (s32[1,1,1,6,64]{4,2,3,1,0:T(1,128)S(1)}, s32[1,1,1,6,64]{4,2,3,1,0:T(1,128)}, u32[]{:S(2)}) copy-start(s32[1,1,1,6,64]{4,2,3,1,0:T(1,128)} %param.13) | copy-start | bytes 4612
  2.0 0.7 %copy-start.8 = (f32[1,1,1,3,512]{4,2,3,1,0:T(1,128)S(1)}, f32[1,1,1,3,512]{4,2,3,1,0:T(1,128)}, u32[]{:S(2)}) copy-start(f32[1,1,1,3,512]{4,2,3,1,0:T(1,128)} %param.12) | copy-start | bytes 18436
  2.7 0.7 %copy-start.3 = (f32[1,1,1,512]{3,2,1,0:T(1,128)S(1)}, f32[1,1,1,512]{3,2,1,0:T(1,128)}, u32[]{:S(2)}) copy-start(f32[1,1,1,512]{3,2,1,0:T(1,128)} %param.14) | copy-start | bytes 6148
  2.7 0.7 %copy-start.4 = (f32[1,1,1,4,64]{4,3,2,1,0:T(4,128)S(1)}, f32[1,1,1,4,64]{4,3,2,1,0:T(4,128)}, u32[]{:S(2)}) copy-start(f32[1,1,1,4,64]{4,3,2,1,0:T(4,128)} %param.15) | copy-start | bytes 3076
  2.7 0.7 %copy-start.5 = (f32[1,1,4,64]{3,2,1,0:T(4,128)S(1)}, f32[1,1,4,64]{3,2,1,0:T(4,128)}, u32[]{:S(2)}) copy-start(f32[1,1,4,64]{3,2,1,0:T(4,128)} %param.18) | copy-start | bytes 3076
  2.7 0.7 %copy-start.6 = (f32[4,64]{1,0:T(4,128)S(1)}, f32[4,64]{1,0:T(4,128)}, u32[]{:S(2)}) copy-start(f32[4,64]{1,0:T(4,128)} %global_first.1) | copy-start | bytes 3076
  2.7 0.7 %copy-start.7 = (f32[3,64]{1,0:T(4,128)S(1)}, f32[3,64]{1,0:T(4,128)}, u32[]{:S(2)}) copy-start(f32[3,64]{1,0:T(4,128)} %global_last.1) | copy-start | bytes 2308
  3.5 0.8 %copy-start = (f32[1,1,1,2,64,64]{5,4,3,2,1,0:T(8,128)S(1)}, f32[1,1,1,2,64,64]{5,4,3,2,1,0:T(8,128)}, u32[]{:S(2)}) copy-start(f32[1,1,1,2,64,64]{5,4,3,2,1,0:T(8,128)} %param.16) | copy-start | bytes 98308
  4.3 0.8 %copy-start.1 = (f32[1,1,2,64,64]{4,3,2,1,0:T(8,128)S(1)}, f32[1,1,2,64,64]{4,3,2,1,0:T(8,128)}, u32[]{:S(2)}) copy-start(f32[1,1,2,64,64]{4,3,2,1,0:T(8,128)} %param.19) | copy-start | bytes 98308
  5.1 0.8 %copy-start.2 = (f32[2,64,64]{2,1,0:T(8,128)S(1)}, f32[2,64,64]{2,1,0:T(8,128)}, u32[]{:S(2)}) copy-start(f32[2,64,64]{2,1,0:T(8,128)} %global_mid.1) | copy-start | bytes 98308
where the time goes:
time: 52.2 us; the launch traced here: 51.9 us
  Pallas kernels  38.2 us (73%)
  local copies, waits for them, and re-layouts  11.2 us (21%)
  between operations  2.46 us (5%)
    pallas_call x1, Pallas kernels, step(): pl.pallas_call(functools.partial(kernel, sizes, chunk), out_shape=[jax.Sh...  38.2 us
    unnamed x38, local copies, waits for them, and re-layouts  11.2 us

commit v1 on v0

v1 whole, which is shorter than its diff:
```python
import functools

import jax
import jax.numpy as jnp
from jax import lax
from jax.experimental import pallas as pl
from jax.experimental.pallas import tpu as pltpu
from jax.sharding import PartitionSpec as P

MESH = pl.DeviceIdType.MESH
AXES = ("gx", "gy", "gz")
f32, bf16 = jnp.float32, jnp.bfloat16
wave_square = 4.0
inverse_depth = 8.0
TILES = 9
NT = (((1,), (1,)), ((), ()))


def split(value):
    high = value.astype(bf16)
    return high, (value - high.astype(f32)).astype(bf16)


def three(value):
    first = value.astype(bf16)
    rest = value - first.astype(f32)
    second = rest.astype(bf16)
    return first, second, (rest - second.astype(f32)).astype(bf16)


def left(matrix):
    high = matrix.astype(bf16).astype(f32)
    return jnp.concatenate([high, high, matrix - high], 1).astype(bf16)


def right(high, low):
    return jnp.concatenate([high, low, high], 0)


def dot(a, b):
    return jnp.dot(a, b, preferred_element_type=f32)


def dot_nt(a, b):
    return lax.dot_general(a, b, NT, preferred_element_type=f32)


def window(depth, facing):
    square = depth * depth
    smooth = depth * (15.0 - 10.0 * square + 3.0 * square * square) / 8.0
    blend = 0.5 * (1.0 - smooth)
    slope = (0.5 * inverse_depth * 15.0 / 8.0) * facing * (1.0 - square) * (1.0 - square)
    bend = (0.5 * inverse_depth * inverse_depth * 7.5) * depth * (1.0 - square)
    return blend, slope, bend


def kernel(sizes, *refs):
    (
        points_hbm,
        band_hbm,
        source_hbm,
        fine_first_hbm,
        fine_mid_hbm,
        fine_last_hbm,
        column_first_hbm,
        column_mid_hbm,
        column_last_hbm,
        global_first_hbm,
        global_mid_hbm,
        global_last_hbm,
        residual_out,
        fine_first_out,
        fine_mid_out,
        fine_last_out,
        column_first_out,
        column_mid_out,
        column_last_out,
        global_first_out,
        global_mid_out,
        global_last_out,
        loss_out,
        points,
        band,
        source,
        fine_first,
        fine_mid,
        fine_last,
        column_first,
        column_mid,
        column_last,
        global_first,
        global_mid,
        global_last,
        nets,
        grads,
        f1,
        f2,
        b2,
        b1h,
        b1s,
        b1p,
        cols,
        xp,
        xpb,
        alpha,
        x0,
        x1,
        h0s,
        a1,
        a2,
        res,
        xf,
        xfb,
        falpha,
        fcols,
        fx0,
        fx1,
        fh0s,
        fa1,
        fa2,
        fdelta,
        hot,
        back,
        tiles,
        levels,
        summed,
        columns,
        load_sem,
        halo_send,
        halo_recv,
        back_send,
        back_recv,
        tile_send,
        tile_recv,
        level_send,
        level_recv,
        share_send,
        share_recv,
        column_send,
        column_recv,
    ) = refs
    me = tuple(lax.axis_index(axis) for axis in AXES)
    count = points.shape[2]
    slots = band.shape[2]
    pair = 2 * slots
    near = 6 * slots
    plane = sizes[0] * sizes[1]
    stride = plane // TILES
    here = me[0] * sizes[1] + me[1]
    reducer = (lax.rem(here, stride) == 0) & (here // stride < TILES)
    my_rows = pl.ds(pl.multiple_of(8 * lax.rem(here // stride, TILES), 8), 8)

    def peer(axis, offset):
        other = list(me)
        other[axis] = lax.rem(me[axis] + (offset + sizes[axis]), sizes[axis])
        return tuple(other)

    def in_plane(place):
        return (place // sizes[1], lax.rem(place, sizes[1]), me[2])

    barrier = pltpu.get_barrier_semaphore()
    friends = [in_plane(lax.rem(here + offset, plane)) for offset in range(1, plane)]
    friends += [peer(2, offset) for offset in range(1, sizes[2])]
    for friend in friends:
        pl.semaphore_signal(barrier, inc=1, device_id=friend, device_id_type=MESH)

    loads = [
        pltpu.make_async_copy(refs[k], refs[23 + k], load_sem.at[k])
        for k in (4, 3, 5, 0, 1, 2, 10, 9, 11, 7, 6, 8)
    ]
    for load in loads:
        load.start()

    def pack(net, first, mid, last):
        nets[net, 0:64, :] = jnp.concatenate([mid[0], mid[1]], 1)
        nets[net, 64:68, 0:64] = first[...]
        for k in range(3):
            nets[net, 68 + k : 69 + k, 0:64] = last[k] if len(last.shape) == 3 else last[k : k + 1, :]
        nets[net, 71:72, 0:64] = jnp.zeros((1, 64), f32)
        nets[net, 64:72, 64:128] = jnp.zeros((8, 64), f32)

    for load in loads[:3]:
        load.wait()
    pack(2, fine_first, fine_mid, fine_last)
    for load in loads[3:]:
        load.wait()
    pack(1, column_first, column_mid, column_last)
    pack(0, global_first, global_mid, global_last)

    def halo(face):
        axis, up = face // 2, face % 2
        return pltpu.make_async_remote_copy(
            src_ref=nets.at[2],
            dst_ref=nets.at[3 + (face ^ 1)],
            send_sem=halo_send.at[face],
            recv_sem=halo_recv.at[face ^ 1],
            device_id=peer(axis, 2 * up - 1),
            device_id_type=MESH,
        )

    faces = [face for face in range(6) if sizes[face // 2] > 1]
    place = [me[axis].astype(f32) for axis in range(3)]

    def affine(net):
        scale, shift = [], []
        for axis in range(3):
            fitted_scale = 2.0 / sizes[axis]
            fitted_shift = (2.0 * place[axis] + 1.0) * (1.0 / sizes[axis]) - 1.0
            fitted = (net == 0) if axis < 2 else (net <= 1)
            scale.append(jnp.where(fitted, fitted_scale, 2.0))
            shift.append(jnp.where(fitted, fitted_shift, 0.0))
        return scale, shift

    def face_affine(face):
        shift = [0.0, 0.0, 0.0]
        shift[face // 2] = 2.0 - 4.0 * (face % 2)
        return [2.0, 2.0, 2.0], shift

    def prepare_forward(net, scale, shift):
        mats = nets[net, 0:64, :]
        rows = nets[net, 64:72, :]
        turned = rows.T
        m1 = mats[:, 0:64]
        row = [scale[d] * rows[d : d + 1, 0:64] for d in range(3)]
        square = -2.0 * (row[0] * row[0] + row[1] * row[1] + row[2] * row[2])
        bias = turned[0:64, 3:4]
        for d in range(3):
            bias = bias + shift[d] * turned[0:64, d : d + 1]
        f1[net, 0:64, :] = left(m1)
        for d in range(3):
            f1[net, 64 * (d + 1) : 64 * (d + 2), :] = left(m1 * row[d])
        f1[net, 256:320, :] = left(m1 * square)
        f2[net] = left(mats[:, 64:128])
        lane = lax.broadcasted_iota(jnp.int32, (64, 8), 1)
        kept = turned[0:64, 0:8]
        for d in range(3):
            kept = jnp.where(lane == d, scale[d] * kept, kept)
        cols[net, :, 0:8] = jnp.where(lane == 3, bias, kept)

    def prepare_backward(net):
        turned = nets[net, 0:64, :].T
        m1t = turned[0:64]
        b1h[net] = left(m1t)
        col = [cols[net, :, d : d + 1] for d in range(3)]
        for d in range(3):
            b1s[net, :, 192 * d : 192 * (d + 1)] = left(m1t * col[d])
        b1p[net] = left(m1t * (-2.0 * (col[0] * col[0] + col[1] * col[1] + col[2] * col[2])))
        b2[net] = left(turned[64:128])

    lane_ones = jnp.ones((1, count), f32)
    for d in range(3):
        xp[d : d + 1, :] = points[d]
    xp[3:4, :] = lane_ones
    xp[4:8, :] = jnp.zeros((4, count), f32)
    x_terms = three(xp[...])
    xpb[...] = jnp.zeros(xpb.shape, bf16)
    xpb[0:16, :] = jnp.concatenate([x_terms[0].astype(f32), x_terms[1].astype(f32)], 0).astype(bf16)

    def present(face):
        axis = face // 2
        there = me[axis] < sizes[axis] - 1 if face % 2 else me[axis] > 0
        return jnp.where(there, 1.0, 0.0).astype(f32)

    inside = lane_ones
    curve = jnp.zeros((1, count), f32)
    for axis in range(3):
        along = points[axis]
        upper = along > 0.0
        facing = jnp.where(upper, 1.0, -1.0)
        depth = jnp.minimum((0.5 - jnp.abs(along)) * inverse_depth, 1.0)
        exists = jnp.where(upper, present(2 * axis + 1), present(2 * axis))
        blend, slope, bend = window(depth, facing)
        inside = inside - exists * blend
        curve = curve - exists * bend
        alpha[2, 1 + axis : 2 + axis, :] = -2.0 * exists * slope
    alpha[2, 0:1, :] = wave_square * inside + curve
    alpha[2, 4:5, :] = inside
    for net in (0, 1):
        alpha[net, 0:1, :] = wave_square * lane_ones
        alpha[net, 1:4, :] = jnp.zeros((3, count), f32)
        alpha[net, 4:5, :] = lane_ones

    if friends:
        pl.semaphore_wait(barrier, len(friends))
    for face in faces:
        halo(face).start()

    near_lane = lax.broadcasted_iota(jnp.int32, (1, near), 1)
    face_of = near_lane // slots
    lower = lax.rem(face_of, 2) == 0
    stacked = jnp.concatenate([term.astype(f32) for term in x_terms], 0).astype(bf16)
    point_id = lax.broadcasted_iota(jnp.int32, (count, near), 0)
    listed = jnp.concatenate([band[face] for face in range(6)], 1)
    hot[...] = jnp.where(point_id == listed, 1.0, 0.0).astype(bf16)
    taken = dot(stacked, hot[...])
    taken = taken[0:8] + taken[8:16] + taken[16:24]
    xf[...] = taken
    high, low = split(taken)
    xfb[...] = jnp.zeros(xfb.shape, bf16)
    xfb[0:16, :] = jnp.concatenate([high.astype(f32), low.astype(f32)], 0).astype(bf16)
    facing = jnp.where(lower, -1.0, 1.0)
    axis_of = face_of // 2
    along = jnp.where(axis_of == 0, taken[0:1], jnp.where(axis_of == 1, taken[1:2], taken[2:3]))
    exists = jnp.zeros((1, near), f32)
    for face in range(6):
        exists = jnp.where(face_of == face, present(face), exists)
    depth = jnp.minimum((0.5 - facing * along) * inverse_depth, 1.0)
    blend, slope, bend = window(depth, facing)
    falpha[0:1, :] = exists * (wave_square * blend + bend)
    for d in range(3):
        falpha[1 + d : 2 + d, :] = jnp.where(axis_of == d, 2.0 * exists * slope, 0.0)
    falpha[4:5, :] = exists * blend

    def tanh_layer(z, f, m):
        h = jnp.tanh(z)
        s = 1.0 - h * h
        q = f[0] * f[0] + f[1] * f[1] + f[2] * f[2]
        return h, s, q, m - 2.0 * h * q

    def forward(get, x, al, mm, keep0, keep1, keep2):
        z = get(0) * x[0:1] + get(1) * x[1:2] + get(2) * x[2:3] + get(3)
        h = jnp.tanh(z)
        s = 1.0 - h * h
        p = h * s
        parts = [split(v) for v in (h, s, p)]
        keep0(h, parts)
        m1h = mm(f1, 0, 64, [right(*parts[0])])[0]
        m1f = mm(f1, 64, 256, [right(*parts[1])])[0]
        m1l = mm(f1, 256, 320, [right(*parts[2])])[0]
        f = [m1f[64 * d : 64 * (d + 1)] for d in range(3)]
        h, s, q, w = tanh_layer(m1h + get(4), f, m1l)
        parts = [split(v) for v in (h, s * f[0], s * f[1], s * f[2], s * w)]
        keep1((h, f[0], f[1], f[2], q, w), parts)
        out = mm(f2, 0, 64, [right(*part) for part in parts])
        f = out[1:4]
        h, s, q, w = tanh_layer(out[0] + get(5), f, out[4])
        u = al[1:2] * f[0] + al[2:3] * f[1] + al[3:4] * f[2] + al[4:5] * w
        c = al[0:1] * h + s * u
        keep2((h, f[0], f[1], f[2], q, u, c))
        return jnp.sum(get(6) * c, axis=0, keepdims=True)

    def backward(get, al, delta, mm, lane_sum, saved0, saved1, saved2):
        h, fa, fb, fc, q, u, c = saved2
        f = (fa, fb, fc)
        dlast = lane_sum(delta * c)
        e = get(6) * delta
        s = 1.0 - h * h
        es = e * s
        gm = es * al[4:5]
        k = 4.0 * h * gm
        gf = [es * al[1 + d : 2 + d] - k * f[d] for d in range(3)]
        gz = (e * al[0:1] - 2.0 * (q * gm + h * (e * u))) * s
        dbias1 = lane_sum(gz)
        g2 = [split(v) for v in (gz, gf[0], gf[1], gf[2], gm)]
        oh, oa, ob, oc, ol = mm(b2, 0, 64, [right(*part) for part in g2])
        o = (oa, ob, oc)
        h, fa, fb, fc, q, w = saved1
        f = (fa, fb, fc)
        s = 1.0 - h * h
        gm = ol * s
        k = 4.0 * h * gm
        gf = [o[d] * s - k * f[d] for d in range(3)]
        gs = o[0] * f[0] + o[1] * f[1] + o[2] * f[2] + ol * w
        gz = (oh - 2.0 * (q * gm + h * gs)) * s
        dbias0 = lane_sum(gz)
        g1 = [split(v) for v in (gz, gf[0], gf[1], gf[2], gm)]
        oh = mm(b1h, 0, 64, [right(*g1[0])])[0]
        os = mm(b1s, 0, 64, [jnp.concatenate([right(*part) for part in g1[1:4]], 0)])[0]
        op = mm(b1p, 0, 64, [right(*g1[4])])[0]
        h = saved0
        s = 1.0 - h * h
        gz = (oh + op * s - 2.0 * h * (os + op * h)) * s
        return g2, g1, split(gz), dlast, dbias1, dbias0

    def fold(product):
        return product[0:64] + product[64:128]

    def finish(net, scale, shift, dm2, ah, af, al, pts, dlast, dbias1, dbias0, extra):
        lane = lax.broadcasted_iota(jnp.int32, (64, 128), 1)
        pts = jnp.where(lane == 4, dbias0, pts)
        pts = jnp.where(lane == 5, dbias1, pts)
        pts = jnp.where(lane == 6, dlast, pts)
        turned = pts.T
        sums = turned[0:8] + turned[8:16]
        m1 = nets[net, 0:64, 0:64]
        rows = nets[net, 64:72, 0:64]
        row = [scale[d] * rows[d : d + 1] for d in range(3)]
        square = row[0] * row[0] + row[1] * row[1] + row[2] * row[2]
        dsquare = -2.0 * jnp.sum(m1 * al, axis=0, keepdims=True)
        dm1 = ah - 2.0 * (al * square)
        first = []
        for d in range(3):
            dm1 = dm1 + af[d] * row[d]
            slope = sums[d : d + 1] + jnp.sum(m1 * af[d], axis=0, keepdims=True) + 2.0 * row[d] * dsquare
            first.append(scale[d] * slope + shift[d] * sums[3:4])
        grads[net, 0:64, :] = jnp.concatenate([dm1, dm2], 1)
        grads[net, 64:72, 0:64] = jnp.concatenate(first + [sums[3:7], extra], 0)
        grads[net, 64:72, 64:128] = jnp.zeros((8, 64), f32)

    def wide_tools(net):
        def get(k):
            return cols[net, :, k : k + 1]

        def mm(ref, low, high, streams):
            out = dot(ref[net, low:high, :], jnp.concatenate(streams, 1))
            return [out[:, count * k : count * (k + 1)] for k in range(len(streams))]

        return get, mm

    def row_sums(value):
        return jnp.sum(value, axis=1, keepdims=True)

    def forward_wide(net):
        get, mm = wide_tools(net)

        def keep_parts(ref, parts):
            for k, part in enumerate(parts):
                ref[net, k, 0:64, :] = part[0]
                ref[net, k, 64:128, :] = part[1]

        def keep0(h, parts):
            h0s[net] = h
            keep_parts(x0, parts)

        def keep1(values, parts):
            for k, value in enumerate(values):
                a1[net, k] = value
            keep_parts(x1, parts)

        def keep2(values):
            for k, value in enumerate(values):
                a2[net, k] = value

        res[0:1, :] = res[0:1, :] + forward(get, xp[...], alpha[net], mm, keep0, keep1, keep2)

    def sides(value, low=0):
        return value[:, low : low + 64] + value[:, low + 64 : low + 128]

    def both(part):
        return jnp.concatenate(part, 0)

    def backward_wide(net, extra):
        get, mm = wide_tools(net)
        g2, g1, g0, dlast, dbias1, dbias0 = backward(
            get,
            alpha[net],
            res[1:2, :],
            mm,
            row_sums,
            h0s[net],
            [a1[net, k] for k in range(6)],
            [a2[net, k] for k in range(7)],
        )
        dm2 = dot_nt(
            jnp.concatenate([both(g) for g in g2], 1),
            jnp.concatenate([x1[net, k] for k in range(5)], 1),
        )
        ah = dot_nt(both(g1[0]), x0[net, 0])
        af = dot_nt(jnp.concatenate([both(g) for g in g1[1:4]], 0), x0[net, 1])
        al = dot_nt(both(g1[4]), x0[net, 2])
        pts = fold(dot_nt(both(g0), xpb[...]))
        af = [sides(fold(af[128 * d : 128 * (d + 1)])) for d in range(3)]
        scale, shift = affine(net)
        dm2, ah, al = [sides(fold(value)) for value in (dm2, ah, al)]
        finish(net, scale, shift, dm2, ah, af, al, pts, dlast, dbias1, dbias0, extra)

    half = lax.broadcasted_iota(jnp.int32, (1, pair), 1) < slots
    first_half = jnp.where(lower, 1.0, 0.0).astype(bf16)
    second_half = jnp.where(lower, 0.0, 1.0).astype(bf16)

    def face_get(k):
        return fcols[k]

    def face_mm(ref, low, high, streams):
        rows = high - low
        number = len(streams)
        mask = (lax.broadcasted_iota(jnp.int32, (1, number * pair), 1) & (pair - 1)) < slots
        pieces = []
        for axis in range(3):
            net = 3 + 2 * axis
            span = slice(axis * pair, (axis + 1) * pair)
            lhs = jnp.concatenate([ref[net, low:high, :], ref[net + 1, low:high, :]], 0)
            out = dot(lhs, jnp.concatenate([stream[:, span] for stream in streams], 1))
            out = jnp.where(mask, out[0:rows], out[rows : 2 * rows])
            pieces.append([out[:, pair * k : pair * (k + 1)] for k in range(number)])
        return [jnp.concatenate([piece[k] for piece in pieces], 1) for k in range(number)]

    def half_sums(value):
        return [
            row_sums(jnp.where(half if face % 2 == 0 else ~half, value[:, pair * (face // 2) : pair * (face // 2 + 1)], 0.0))
            for face in range(6)
        ]

    def forward_faces():
        def keep_parts(ref, parts):
            for k, part in enumerate(parts):
                ref[k, 0:64, :] = part[0] * first_half
                ref[k, 64:128, :] = part[1] * first_half
                ref[k, 128:192, :] = part[0] * second_half
                ref[k, 192:256, :] = part[1] * second_half

        def keep0(h, parts):
            fh0s[...] = h
            keep_parts(fx0, parts)

        def keep1(values, parts):
            for k, value in enumerate(values):
                fa1[k] = value
            keep_parts(fx1, parts)

        def keep2(values):
            for k, value in enumerate(values):
                fa2[k] = value

        row = forward(face_get, xf[...], falpha[...], face_mm, keep0, keep1, keep2)
        terms = jnp.concatenate([term.astype(f32) for term in three(row)] + [jnp.zeros((5, near), f32)], 0)
        spread = dot_nt(terms.astype(bf16), hot[...])
        res[0:1, :] = res[0:1, :] + (spread[0:1] + spread[1:2] + spread[2:3])

    def backward_faces():
        g2, g1, g0, dlast, dbias1, dbias0 = backward(
            face_get,
            falpha[...],
            fdelta[0:1, :],
            face_mm,
            half_sums,
            fh0s[...],
            [fa1[k] for k in range(6)],
            [fa2[k] for k in range(7)],
        )
        for axis in range(3):
            span = slice(axis * pair, (axis + 1) * pair)

            def cut(part):
                return jnp.concatenate([part[0][:, span], part[1][:, span]], 0)

            dm2 = fold(
                dot_nt(
                    jnp.concatenate([cut(g) for g in g2], 1),
                    jnp.concatenate([fx1[k, :, span] for k in range(5)], 1),
                )
            )
            ah = fold(dot_nt(cut(g1[0]), fx0[0, :, span]))
            af = dot_nt(jnp.concatenate([cut(g) for g in g1[1:4]], 0), fx0[1, :, span])
            af = [fold(af[128 * d : 128 * (d + 1)]) for d in range(3)]
            al = fold(dot_nt(cut(g1[4]), fx0[2, :, span]))
            for side in range(2):
                face = 2 * axis + side
                kept = (first_half if side == 0 else second_half)[:, span]
                pts = fold(dot_nt(cut(g0), xfb[:, span] * kept))
                scale, shift = face_affine(face)
                finish(
                    3 + face,
                    scale,
                    shift,
                    sides(dm2, 128 * side),
                    sides(ah, 128 * side),
                    [sides(v, 128 * side) for v in af],
                    sides(al, 128 * side),
                    pts,
                    dlast[face],
                    dbias1[face],
                    dbias0[face],
                    jnp.zeros((1, 64), f32),
                )

    def total(ref, number):
        value = ref[0]
        for k in range(1, number):
            value = value + ref[k]
        return value

    def tile_copy(tile):
        return pltpu.make_async_remote_copy(
            src_ref=grads.at[0, 8 * tile : 8 * tile + 8, :],
            dst_ref=tiles.at[here],
            send_sem=tile_send.at[tile],
            recv_sem=tile_recv.at[here],
            device_id=(tile * stride // sizes[1], tile * stride % sizes[1], me[2]),
            device_id_type=MESH,
        )

    def tile_arrival(sender):
        return pltpu.make_async_remote_copy(
            src_ref=grads.at[0, 0:8, :],
            dst_ref=tiles.at[sender],
            send_sem=tile_send.at[0],
            recv_sem=tile_recv.at[sender],
            device_id=in_plane(sender),
            device_id_type=MESH,
        )

    def along_z(source_ref, ref, send, recv, offset, sender):
        return pltpu.make_async_remote_copy(
            src_ref=source_ref,
            dst_ref=ref.at[sender],
            send_sem=send.at[offset],
            recv_sem=recv.at[sender],
            device_id=peer(2, offset),
            device_id_type=MESH,
        )

    def level_copy(offset, arriving):
        sender = lax.rem(me[2] + (sizes[2] - offset), sizes[2]) if arriving else me[2]
        return along_z(levels.at[me[2]], levels, level_send, level_recv, offset, sender)

    def column_copy(offset, arriving):
        sender = lax.rem(me[2] + (sizes[2] - offset), sizes[2]) if arriving else me[2]
        return along_z(grads.at[1], columns, column_send, column_recv, offset, sender)

    def share_copy(offset):
        return pltpu.make_async_remote_copy(
            src_ref=summed.at[my_rows, :],
            dst_ref=summed.at[my_rows, :],
            send_sem=share_send.at[offset],
            recv_sem=share_recv.at[lax.rem(here // stride, TILES)],
            device_id=in_plane(lax.rem(here + offset, plane)),
            device_id_type=MESH,
        )

    def share_arrival(tile):
        rows = summed.at[8 * tile : 8 * tile + 8, :]
        return pltpu.make_async_remote_copy(
            src_ref=rows,
            dst_ref=rows,
            send_sem=share_send.at[0],
            recv_sem=share_recv.at[tile],
            device_id=in_plane(tile * stride),
            device_id_type=MESH,
        )

    def send_back(face):
        axis, up = face // 2, face % 2
        return pltpu.make_async_remote_copy(
            src_ref=grads.at[3 + face],
            dst_ref=back.at[face ^ 1],
            send_sem=back_send.at[face],
            recv_sem=back_recv.at[face ^ 1],
            device_id=peer(axis, 2 * up - 1),
            device_id_type=MESH,
        )

    def give(value, first_ref, mid_ref, last_ref):
        mid_ref[0] = value[0:64, 0:64]
        mid_ref[1] = value[0:64, 64:128]
        first_ref[...] = value[64:68, 0:64]
        for k in range(3):
            if len(last_ref.shape) == 3:
                last_ref[k] = value[68 + k : 69 + k, 0:64]
            else:
                last_ref[k : k + 1, :] = value[68 + k : 69 + k, 0:64]

    res[0:1, :] = -source[...]

    def wide(net, carry):
        prepare_forward(net, *affine(net))
        forward_wide(net)
        return carry

    lax.fori_loop(0, 3, wide, 0)
    prepare_backward(0)
    for face in faces:
        halo(face).wait()
    for face in range(6):
        prepare_forward(3 + face, *face_affine(face))
    for k in range(7):
        fcols[k] = jnp.concatenate(
            [
                jnp.where(half, cols[3 + 2 * axis, :, k : k + 1], cols[4 + 2 * axis, :, k : k + 1])
                for axis in range(3)
            ],
            1,
        )
    forward_faces()

    residual = res[0:1, :]
    residual_out[...] = residual
    delta = residual * (1.0 / count)
    res[1:2, :] = delta
    loss = jnp.sum(residual * residual, axis=1, keepdims=True) * (0.5 / count)

    first_lane = lax.broadcasted_iota(jnp.int32, (1, 64), 1) == 0
    backward_wide(0, jnp.where(first_lane, loss, 0.0))
    for tile in range(TILES):
        pl.when(here != tile * stride)(tile_copy(tile).start)

    prepare_backward(1)
    backward_wide(1, jnp.zeros((1, 64), f32))
    columns[me[2]] = grads[1]
    for offset in range(1, sizes[2]):
        column_copy(offset, False).start()

    terms = jnp.concatenate([term.astype(f32) for term in three(delta)] + [jnp.zeros((5, count), f32)], 0)
    taken = dot(terms.astype(bf16), hot[...])
    fdelta[0:1, :] = taken[0:1] + taken[1:2] + taken[2:3]

    def prepare_rest(net, carry):
        prepare_backward(net)
        return carry

    lax.fori_loop(2, 9, prepare_rest, 0)
    backward_faces()
    for face in faces:
        send_back(face).start()

    @pl.when(reducer)
    def _():
        tiles[here] = grads[0, my_rows, :]
        for offset in range(1, plane):
            tile_arrival(lax.rem(here + offset, plane)).wait_recv()
        levels[me[2]] = total(tiles, plane)
        for offset in range(1, sizes[2]):
            level_copy(offset, False).start()

    backward_wide(2, jnp.zeros((1, 64), f32))

    for face in faces:
        send_back(face).wait()
    give(grads[2] + total(back, 6), fine_first_out, fine_mid_out, fine_last_out)
    for offset in range(1, sizes[2]):
        column_copy(offset, True).wait_recv()
    give(total(columns, sizes[2]), column_first_out, column_mid_out, column_last_out)

    @pl.when(reducer)
    def _():
        for offset in range(1, sizes[2]):
            level_copy(offset, True).wait_recv()
        summed[my_rows, :] = total(levels, sizes[2])
        for offset in range(1, plane):
            share_copy(offset).start()

    for offset in range(1, sizes[2]):
        column_copy(offset, False).wait_send()
    for tile in range(TILES):
        pl.when(here != tile * stride)(tile_copy(tile).wait_send)
    for tile in range(TILES):
        pl.when(here != tile * stride)(share_arrival(tile).wait_recv)
    value = summed[...]
    give(value, global_first_out, global_mid_out, global_last_out)
    loss_out[...] = value[71:72, 0:1]

    @pl.when(reducer)
    def _():
        for offset in range(1, sizes[2]):
            level_copy(offset, False).wait_send()
        for offset in range(1, plane):
            share_copy(offset).wait_send()


def hand_over(*refs):
    number = len(refs) // 2
    ins, outs, sem = refs[:number], refs[number : 2 * number], refs[2 * number]
    copies = [pltpu.make_async_copy(ins[k], outs[k], sem.at[k]) for k in range(number - 1)]
    for copy in copies:
        copy.start()
    outs[number - 1][...] = ins[number - 1][...]
    for copy in copies:
        copy.wait()


def step(sizes, points, band_index, source, *params):
    count = points.shape[-1]
    slots = band_index.shape[-1]
    near = 6 * slots
    plane = sizes[0] * sizes[1]
    operands = [points.reshape(3, 1, count), band_index.reshape(6, 1, slots), source.reshape(1, count)]
    shapes = [(4, 64), (2, 64, 64), (3, 1, 64)] * 2 + [(4, 64), (2, 64, 64), (3, 64)]
    operands += [param.reshape(shape) for param, shape in zip(params, shapes)]
    outs = [jax.ShapeDtypeStruct(shape, f32) for shape in [(1, count)] + shapes + [(1, 1)]]
    vmem = pltpu.VMEM
    scratch = [vmem(value.shape, value.dtype) for value in operands]
    scratch += [
        vmem((9, 72, 128), f32),
        vmem((9, 72, 128), f32),
        vmem((9, 320, 192), bf16),
        vmem((9, 64, 192), bf16),
        vmem((9, 64, 192), bf16),
        vmem((9, 64, 192), bf16),
        vmem((9, 64, 576), bf16),
        vmem((9, 64, 192), bf16),
        vmem((9, 64, 128), f32),
        vmem((8, count), f32),
        vmem((128, count), bf16),
        vmem((3, 8, count), f32),
        vmem((3, 3, 128, count), bf16),
        vmem((3, 5, 128, count), bf16),
        vmem((3, 64, count), f32),
        vmem((3, 6, 64, count), f32),
        vmem((3, 7, 64, count), f32),
        vmem((8, count), f32),
        vmem((8, near), f32),
        vmem((128, near), bf16),
        vmem((8, near), f32),
        vmem((7, 64, near), f32),
        vmem((3, 256, near), bf16),
        vmem((5, 256, near), bf16),
        vmem((64, near), f32),
        vmem((6, 64, near), f32),
        vmem((7, 64, near), f32),
        vmem((8, near), f32),
        vmem((count, near), bf16),
        vmem((6, 72, 128), f32),
        vmem((plane, 8, 128), f32),
        vmem((sizes[2], 8, 128), f32),
        vmem((72, 128), f32),
        vmem((sizes[2], 72, 128), f32),
    ]
    dma = pltpu.SemaphoreType.DMA
    scratch += [dma((12,))] + [dma((6,))] * 4
    scratch += [dma((number,)) for number in (TILES, plane, sizes[2], sizes[2], plane, TILES, sizes[2], sizes[2])]
    whole = pl.BlockSpec(memory_space=pltpu.VMEM)
    outside = pl.BlockSpec(memory_space=pltpu.HBM)
    results = pl.pallas_call(
        functools.partial(kernel, sizes),
        out_shape=[vmem(value.shape, value.dtype) for value in outs],
        in_specs=[outside] * 12,
        out_specs=[whole] * 11,
        scratch_shapes=scratch,
        compiler_params=pltpu.CompilerParams(
            collective_id=0, has_side_effects=True, vmem_limit_bytes=32 << 20
        ),
        cost_estimate=pl.CostEstimate(flops=500_000_000, bytes_accessed=1_000_000, transcendentals=400_000),
        name="training_step",
    )(*[pltpu.with_memory_space_constraint(value, pltpu.HBM) for value in operands])
    results = pl.pallas_call(
        hand_over,
        out_shape=outs,
        in_specs=[whole] * 11,
        out_specs=[outside] * 10 + [whole],
        scratch_shapes=[dma((10,))],
        compiler_params=pltpu.CompilerParams(vmem_limit_bytes=1 << 20),
        cost_estimate=pl.CostEstimate(flops=0, bytes_accessed=400_000, transcendentals=0),
        name="hand_over",
    )(*results)
    ranks = [params[k].shape for k in range(9)]
    arrays = [results[0].reshape(source.shape)]
    arrays += [value.reshape(shape) for value, shape in zip(results[1:10], ranks)]
    return tuple(arrays) + (results[10].reshape(()),)


def solution(mesh):
    sizes = tuple(mesh.shape[axis] for axis in AXES)
    cell = ("gx", "gy", "gz")
    column = ("gx", "gy")
    in_specs = (P(*cell, None, None), P(*cell, None, None), P(*cell, None))
    nets_specs = (
        (P(*cell, None, None), P(*cell, None, None, None), P(*cell, None, None))
        + (P(*column, None, None), P(*column, None, None, None), P(*column, None, None))
        + (P(), P(), P())
    )
    return jax.shard_map(
        functools.partial(step, sizes),
        mesh=mesh,
        in_specs=in_specs + nets_specs,
        out_specs=(P(*cell, None),) + nets_specs + (P(),),
        check_vma=False,
    )
```

time: 52.2 us -> 38.5 us (0.74)
  local copies, waits for them, and re-layouts: 11.2 us -> 0 us
  between operations: 2.46 us -> 0.66 us
    unnamed x38 -> x0, local copies, waits for them, and re-layouts: 11.2 us -> none
    pallas_call x1 -> x2, Pallas kernels: 38.2 us -> 37.7 us  [the longest x1 35.8 us: step(): pl.pallas_call(functools.partial(kernel, sizes), out_shape=[vmem(value.sh...]
where the time goes in v1:
time: 38.5 us; the launch traced here: 38.4 us
  Pallas kernels  37.7 us (98%)
  between operations  0.66 us (2%)
    pallas_call x1, Pallas kernels, step(): pl.pallas_call(functools.partial(kernel, sizes), out_shape=[vmem(value.sh...  35.8 us
    pallas_call x1, Pallas kernels, step(): pl.pallas_call(hand_over, out_shape=outs, in_specs=[whole] * 11, out_spec...  1.93 us

profile of v1, /device:TPU:1, one launch (start us, length us, event | category | flops | bytes accessed | tf_op | source)
XLA Modules:
  0.0 38.4 jit_solution(7344035196847563380)
XLA Ops:
  0.6 35.8 %training_step.1 = (f32[1,512]{1,0:T(1,128)S(1)}, f32[4,64]{1,0:T(4,128)S(1)}, f32[2,64,64]{2,1,0:T(8,128)S(1)}, f32[3,1,64]{2,1,0:T(1,128)S(1)}, f32[4,64]{1,0:...) custom-call(f32[3,1,512]{2,1,0:T(1,128)} %bitcast.25, ...), custom_call_target="tpu_custom_call" | custom-call | flops 500000000 | bytes 1000000 | tf_op jit(solution)/shard_map/training_step/pallas_call | solution.py:813
  36.5 1.9 %hand_over.1 = (f32[1,512]{1,0:T(1,128)}, f32[4,64]{1,0:T(4,128)}, f32[2,64,64]{2,1,0:T(8,128)}, f32[3,1,64]{2,1,0:T(1,128)}, f32[4,64]{1,0:T(4,128)}, /*index=5...) custom-call(f32[1,512]{1,0:T(1,128)S(1)} %get-tuple-element.33.refs_, ...), custom_call_target="tpu_custom_call" | custom-call | bytes 400000 | tf_op jit(solution)/shard_map/hand_over/pallas_call | solution.py:825

commit v2 on v1

--- a/solution.py
+++ b/solution.py
@@ -52,6 +52,25 @@
     slope = (0.5 * inverse_depth * 15.0 / 8.0) * facing * (1.0 - square) * (1.0 - square)
     bend = (0.5 * inverse_depth * inverse_depth * 7.5) * depth * (1.0 - square)
     return blend, slope, bend
+
+
+def tile_owners(sizes):
+    chips = (sizes[1] + 1) // 2
+
+    def order(place):
+        x, chip = place // sizes[1], place % sizes[1] // 2
+        return (x + chip + place) % 2, max(min(x, sizes[0] - x), min(chip, chips - chip)), place
+
+    return sorted(range(sizes[0] * sizes[1]), key=order)[:TILES]
+
+
+def far_first(sizes):
+    def distance(offset):
+        x, y = offset
+        return -min(x, sizes[0] - x) - min(y, sizes[1] - y) / 2, x, y
+
+    offsets = [(x, y) for x in range(sizes[0]) for y in range(sizes[1]) if x or y]
+    return sorted(offsets, key=distance)
 
 
 def kernel(sizes, *refs):
@@ -125,6 +144,7 @@
         levels,
         summed,
         columns,
+        column_sum,
         load_sem,
         halo_send,
         halo_recv,
@@ -138,6 +158,8 @@
         share_recv,
         column_send,
         column_recv,
+        gather_send,
+        gather_recv,
     ) = refs
     me = tuple(lax.axis_index(axis) for axis in AXES)
     count = points.shape[2]
@@ -145,10 +167,14 @@
     pair = 2 * slots
     near = 6 * slots
     plane = sizes[0] * sizes[1]
-    stride = plane // TILES
     here = me[0] * sizes[1] + me[1]
-    reducer = (lax.rem(here, stride) == 0) & (here // stride < TILES)
-    my_rows = pl.ds(pl.multiple_of(8 * lax.rem(here // stride, TILES), 8), 8)
+    owners = tile_owners(sizes)
+    reducer = here == owners[0]
+    my_tile = jnp.int32(0)
+    for tile in range(1, TILES):
+        reducer = reducer | (here == owners[tile])
+        my_tile = jnp.where(here == owners[tile], tile, my_tile)
+    my_rows = pl.ds(pl.multiple_of(8 * my_tile, 8), 8)
 
     def peer(axis, offset):
         other = list(me)
@@ -242,8 +268,10 @@
         m1t = turned[0:64]
         b1h[net] = left(m1t)
         col = [cols[net, :, d : d + 1] for d in range(3)]
-        for d in range(3):
-            b1s[net, :, 192 * d : 192 * (d + 1)] = left(m1t * col[d])
+        scaled = [m1t * col[d] for d in range(3)]
+        high = [value.astype(bf16).astype(f32) for value in scaled]
+        low = [scaled[d] - high[d] for d in range(3)]
+        b1s[net] = jnp.concatenate(high + high + low, 1).astype(bf16)
         b1p[net] = left(m1t * (-2.0 * (col[0] * col[0] + col[1] * col[1] + col[2] * col[2])))
         b2[net] = left(turned[64:128])
 
@@ -365,7 +393,7 @@
         dbias0 = lane_sum(gz)
         g1 = [split(v) for v in (gz, gf[0], gf[1], gf[2], gm)]
         oh = mm(b1h, 0, 64, [right(*g1[0])])[0]
-        os = mm(b1s, 0, 64, [jnp.concatenate([right(*part) for part in g1[1:4]], 0)])[0]
+        os = mm(b1s, 0, 64, [jnp.concatenate([g1[d][k] for k in (0, 1, 0) for d in (1, 2, 3)], 0)])[0]
         op = mm(b1p, 0, 64, [right(*g1[4])])[0]
         h = saved0
         s = 1.0 - h * h
@@ -576,7 +604,7 @@
             dst_ref=tiles.at[here],
             send_sem=tile_send.at[tile],
             recv_sem=tile_recv.at[here],
-            device_id=(tile * stride // sizes[1], tile * stride % sizes[1], me[2]),
+            device_id=(owners[tile] // sizes[1], owners[tile] % sizes[1], me[2]),
             device_id_type=MESH,
         )
 
@@ -604,17 +632,56 @@
         sender = lax.rem(me[2] + (sizes[2] - offset), sizes[2]) if arriving else me[2]
         return along_z(levels.at[me[2]], levels, level_send, level_recv, offset, sender)
 
-    def column_copy(offset, arriving):
+    layers = -(-TILES // sizes[2])
+
+    def column_copies(offset, arriving):
+        target = lax.rem(me[2] + offset, sizes[2])
         sender = lax.rem(me[2] + (sizes[2] - offset), sizes[2]) if arriving else me[2]
-        return along_z(grads.at[1], columns, column_send, column_recv, offset, sender)
-
-    def share_copy(offset):
+        for layer in range(layers):
+            tile = layer * sizes[2] + (me[2] if arriving else target)
+            rows = pl.ds(pl.multiple_of(8 * lax.rem(tile, TILES), 8), 8)
+            yield tile < TILES, pltpu.make_async_remote_copy(
+                src_ref=grads.at[1, rows, :],
+                dst_ref=columns.at[layer, sender],
+                send_sem=column_send.at[layer, offset],
+                recv_sem=column_recv.at[layer, sender],
+                device_id=peer(2, offset),
+                device_id_type=MESH,
+            )
+
+    def gather_copies(offset, arriving):
+        sender = lax.rem(me[2] + (sizes[2] - offset), sizes[2]) if arriving else me[2]
+        for layer in range(layers):
+            tile = layer * sizes[2] + sender
+            rows = pl.ds(pl.multiple_of(8 * lax.rem(tile, TILES), 8), 8)
+            yield tile < TILES, pltpu.make_async_remote_copy(
+                src_ref=column_sum.at[rows, :],
+                dst_ref=column_sum.at[rows, :],
+                send_sem=gather_send.at[layer, offset],
+                recv_sem=gather_recv.at[layer, sender],
+                device_id=peer(2, offset),
+                device_id_type=MESH,
+            )
+
+    def own_layers():
+        for layer in range(layers):
+            tile = layer * sizes[2] + me[2]
+            yield layer, tile < TILES, pl.ds(pl.multiple_of(8 * lax.rem(tile, TILES), 8), 8)
+
+    def every(copies, arriving, action):
+        for offset in range(1, sizes[2]):
+            for needed, copy in copies(offset, arriving):
+                pl.when(needed)(getattr(copy, action))
+
+    def share_copy(number):
+        x, y = far_first(sizes)[number]
+        target = (lax.rem(me[0] + x, sizes[0]), lax.rem(me[1] + y, sizes[1]), me[2])
         return pltpu.make_async_remote_copy(
             src_ref=summed.at[my_rows, :],
             dst_ref=summed.at[my_rows, :],
-            send_sem=share_send.at[offset],
-            recv_sem=share_recv.at[lax.rem(here // stride, TILES)],
-            device_id=in_plane(lax.rem(here + offset, plane)),
+            send_sem=share_send.at[number],
+            recv_sem=share_recv.at[my_tile],
+            device_id=target,
             device_id_type=MESH,
         )
 
@@ -625,7 +692,7 @@
             dst_ref=rows,
             send_sem=share_send.at[0],
             recv_sem=share_recv.at[tile],
-            device_id=in_plane(tile * stride),
+            device_id=in_plane(owners[tile]),
             device_id_type=MESH,
         )
 
@@ -652,12 +719,9 @@
 
     res[0:1, :] = -source[...]
 
-    def wide(net, carry):
+    for net in range(3):
         prepare_forward(net, *affine(net))
         forward_wide(net)
-        return carry
-
-    lax.fori_loop(0, 3, wide, 0)
     prepare_backward(0)
     for face in faces:
         halo(face).wait()
@@ -682,23 +746,18 @@
     first_lane = lax.broadcasted_iota(jnp.int32, (1, 64), 1) == 0
     backward_wide(0, jnp.where(first_lane, loss, 0.0))
     for tile in range(TILES):
-        pl.when(here != tile * stride)(tile_copy(tile).start)
+        pl.when(here != owners[tile])(tile_copy(tile).start)
 
     prepare_backward(1)
     backward_wide(1, jnp.zeros((1, 64), f32))
-    columns[me[2]] = grads[1]
-    for offset in range(1, sizes[2]):
-        column_copy(offset, False).start()
+    every(column_copies, False, "start")
 
     terms = jnp.concatenate([term.astype(f32) for term in three(delta)] + [jnp.zeros((5, count), f32)], 0)
     taken = dot(terms.astype(bf16), hot[...])
     fdelta[0:1, :] = taken[0:1] + taken[1:2] + taken[2:3]
 
-    def prepare_rest(net, carry):
-        prepare_backward(net)
-        return carry
-
-    lax.fori_loop(2, 9, prepare_rest, 0)
+    for face in range(6):
+        prepare_backward(3 + face)
     backward_faces()
     for face in faces:
         send_back(face).start()
@@ -712,29 +771,44 @@
         for offset in range(1, sizes[2]):
             level_copy(offset, False).start()
 
+    prepare_backward(2)
     backward_wide(2, jnp.zeros((1, 64), f32))
+
+    for layer, needed, rows in own_layers():
+
+        @pl.when(needed)
+        def _(layer=layer, rows=rows):
+            columns[layer, me[2]] = grads[1, rows, :]
+
+    every(column_copies, True, "wait_recv")
+    for layer, needed, rows in own_layers():
+
+        @pl.when(needed)
+        def _(layer=layer, rows=rows):
+            column_sum[rows, :] = total(columns.at[layer], sizes[2])
+
+    every(gather_copies, False, "start")
 
     for face in faces:
         send_back(face).wait()
     give(grads[2] + total(back, 6), fine_first_out, fine_mid_out, fine_last_out)
-    for offset in range(1, sizes[2]):
-        column_copy(offset, True).wait_recv()
-    give(total(columns, sizes[2]), column_first_out, column_mid_out, column_last_out)
 
     @pl.when(reducer)
     def _():
         for offset in range(1, sizes[2]):
             level_copy(offset, True).wait_recv()
         summed[my_rows, :] = total(levels, sizes[2])
-        for offset in range(1, plane):
-            share_copy(offset).start()
-
-    for offset in range(1, sizes[2]):
-        column_copy(offset, False).wait_send()
+        for number in range(plane - 1):
+            share_copy(number).start()
+
+    every(gather_copies, True, "wait_recv")
+    give(column_sum[...], column_first_out, column_mid_out, column_last_out)
+    every(column_copies, False, "wait_send")
+    every(gather_copies, False, "wait_send")
     for tile in range(TILES):
-        pl.when(here != tile * stride)(tile_copy(tile).wait_send)
+        pl.when(here != owners[tile])(tile_copy(tile).wait_send)
     for tile in range(TILES):
-        pl.when(here != tile * stride)(share_arrival(tile).wait_recv)
+        pl.when(here != owners[tile])(share_arrival(tile).wait_recv)
     value = summed[...]
     give(value, global_first_out, global_mid_out, global_last_out)
     loss_out[...] = value[71:72, 0:1]
@@ -743,8 +817,8 @@
     def _():
         for offset in range(1, sizes[2]):
             level_copy(offset, False).wait_send()
-        for offset in range(1, plane):
-            share_copy(offset).wait_send()
+        for number in range(plane - 1):
+            share_copy(number).wait_send()
 
 
 def hand_over(*refs):
@@ -763,6 +837,7 @@
     slots = band_index.shape[-1]
     near = 6 * slots
     plane = sizes[0] * sizes[1]
+    layers = -(-TILES // sizes[2])
     operands = [points.reshape(3, 1, count), band_index.reshape(6, 1, slots), source.reshape(1, count)]
     shapes = [(4, 64), (2, 64, 64), (3, 1, 64)] * 2 + [(4, 64), (2, 64, 64), (3, 64)]
     operands += [param.reshape(shape) for param, shape in zip(params, shapes)]
@@ -803,11 +878,13 @@
         vmem((plane, 8, 128), f32),
         vmem((sizes[2], 8, 128), f32),
         vmem((72, 128), f32),
-        vmem((sizes[2], 72, 128), f32),
+        vmem((layers, sizes[2], 8, 128), f32),
+        vmem((72, 128), f32),
     ]
     dma = pltpu.SemaphoreType.DMA
     scratch += [dma((12,))] + [dma((6,))] * 4
-    scratch += [dma((number,)) for number in (TILES, plane, sizes[2], sizes[2], plane, TILES, sizes[2], sizes[2])]
+    scratch += [dma((number,)) for number in (TILES, plane, sizes[2], sizes[2], plane, TILES)]
+    scratch += [dma((layers, sizes[2]))] * 4
     whole = pl.BlockSpec(memory_space=pltpu.VMEM)
     outside = pl.BlockSpec(memory_space=pltpu.HBM)
     results = pl.pallas_call(

time: 38.5 us -> 36.5 us (0.948)
  Pallas kernels: 37.7 us -> 35.7 us
    pallas_call x1, Pallas kernels: 35.8 us -> 33.8 us  [step(): pl.pallas_call(functools.partial(kernel, sizes), out_shape=[vmem(value.sh...]
where the time goes in v2:
time: 36.5 us; the launch traced here: 36.4 us
  Pallas kernels  35.7 us (98%)
  between operations  0.66 us (2%)
    pallas_call x1, Pallas kernels, step(): pl.pallas_call(functools.partial(kernel, sizes), out_shape=[vmem(value.sh...  33.8 us
    pallas_call x1, Pallas kernels, step(): pl.pallas_call(hand_over, out_shape=outs, in_specs=[whole] * 11, out_spec...  1.93 us

profile of v2, /device:TPU:1, one launch (start us, length us, event | category | flops | bytes accessed | tf_op | source)
XLA Modules:
  0.0 36.4 jit_solution(16716251059896219280)
XLA Ops:
  0.6 33.8 %training_step.1 = (f32[1,512]{1,0:T(1,128)S(1)}, f32[4,64]{1,0:T(4,128)S(1)}, f32[2,64,64]{2,1,0:T(8,128)S(1)}, f32[3,1,64]{2,1,0:T(1,128)S(1)}, f32[4,64]{1,0:...) custom-call(f32[3,1,512]{2,1,0:T(1,128)} %bitcast.25, ...), custom_call_target="tpu_custom_call" | custom-call | flops 500000000 | bytes 1000000 | tf_op jit(solution)/shard_map/training_step/pallas_call | solution.py:890
  34.4 1.9 %hand_over.1 = (f32[1,512]{1,0:T(1,128)}, f32[4,64]{1,0:T(4,128)}, f32[2,64,64]{2,1,0:T(8,128)}, f32[3,1,64]{2,1,0:T(1,128)}, f32[4,64]{1,0:T(4,128)}, /*index=5...) custom-call(f32[1,512]{1,0:T(1,128)S(1)} %get-tuple-element.33.refs_, ...), custom_call_target="tpu_custom_call" | custom-call | bytes 400000 | tf_op jit(solution)/shard_map/hand_over/pallas_call | solution.py:902

commit v3 on v2

--- a/solution.py
+++ b/solution.py
@@ -160,6 +160,7 @@
         column_recv,
         gather_send,
         gather_recv,
+        relay,
     ) = refs
     me = tuple(lax.axis_index(axis) for axis in AXES)
     count = points.shape[2]
@@ -184,11 +185,26 @@
     def in_plane(place):
         return (place // sizes[1], lax.rem(place, sizes[1]), me[2])
 
+    def steps(axes, size):
+        for axis in axes:
+            if size <= sizes[axis] // 2:
+                yield from {(axis, size), (axis, -size % sizes[axis])}
+
+    circles = [sorted(steps((0, 1, 2), 1)), sorted(steps((0, 1, 2), 1)), sorted(steps((0, 1, 2), 2)), sorted(steps((1,), 4))]
     barrier = pltpu.get_barrier_semaphore()
-    friends = [in_plane(lax.rem(here + offset, plane)) for offset in range(1, plane)]
-    friends += [peer(2, offset) for offset in range(1, sizes[2])]
-    for friend in friends:
-        pl.semaphore_signal(barrier, inc=1, device_id=friend, device_id_type=MESH)
+
+    def semaphore_of(number):
+        return relay.at[number - 1] if number else barrier
+
+    def greet(number):
+        for axis, step in circles[number]:
+            pl.semaphore_signal(semaphore_of(number), inc=1, device_id=peer(axis, step), device_id_type=MESH)
+
+    def hear(number):
+        if circles[number]:
+            pl.semaphore_wait(semaphore_of(number), len(circles[number]))
+
+    greet(0)
 
     loads = [
         pltpu.make_async_copy(refs[k], refs[23 + k], load_sem.at[k])
@@ -308,10 +324,10 @@
         alpha[net, 1:4, :] = jnp.zeros((3, count), f32)
         alpha[net, 4:5, :] = lane_ones
 
-    if friends:
-        pl.semaphore_wait(barrier, len(friends))
+    hear(0)
     for face in faces:
         halo(face).start()
+    greet(1)
 
     near_lane = lax.broadcasted_iota(jnp.int32, (1, near), 1)
     face_of = near_lane // slots
@@ -722,6 +738,11 @@
     for net in range(3):
         prepare_forward(net, *affine(net))
         forward_wide(net)
+        if net == 0:
+            hear(1)
+            greet(2)
+    hear(2)
+    greet(3)
     prepare_backward(0)
     for face in faces:
         halo(face).wait()
@@ -745,6 +766,7 @@
 
     first_lane = lax.broadcasted_iota(jnp.int32, (1, 64), 1) == 0
     backward_wide(0, jnp.where(first_lane, loss, 0.0))
+    hear(3)
     for tile in range(TILES):
         pl.when(here != owners[tile])(tile_copy(tile).start)
 
@@ -884,7 +906,7 @@
     dma = pltpu.SemaphoreType.DMA
     scratch += [dma((12,))] + [dma((6,))] * 4
     scratch += [dma((number,)) for number in (TILES, plane, sizes[2], sizes[2], plane, TILES)]
-    scratch += [dma((layers, sizes[2]))] * 4
+    scratch += [dma((layers, sizes[2]))] * 4 + [pltpu.SemaphoreType.REGULAR((3,))]
     whole = pl.BlockSpec(memory_space=pltpu.VMEM)
     outside = pl.BlockSpec(memory_space=pltpu.HBM)
     results = pl.pallas_call(

time: 36.5 us -> 34.7 us (0.951)
  Pallas kernels: 35.7 us -> 33.9 us
    pallas_call x1, Pallas kernels: 33.8 us -> 31.9 us  [step(): pl.pallas_call(functools.partial(kernel, sizes), out_shape=[vmem(value.sh...]
where the time goes in v3:
time: 34.7 us; the launch traced here: 34.5 us
  Pallas kernels  33.9 us (98%)
  between operations  0.66 us (2%)
    pallas_call x1, Pallas kernels, step(): pl.pallas_call(functools.partial(kernel, sizes), out_shape=[vmem(value.sh...  31.9 us
    pallas_call x1, Pallas kernels, step(): pl.pallas_call(hand_over, out_shape=outs, in_specs=[whole] * 11, out_spec...  1.93 us

profile of v3, /device:TPU:1, one launch (start us, length us, event | category | flops | bytes accessed | tf_op | source)
XLA Modules:
  0.0 34.5 jit_solution(13095603127255321132)
XLA Ops:
  0.6 31.9 %training_step.1 = (f32[1,512]{1,0:T(1,128)S(1)}, f32[4,64]{1,0:T(4,128)S(1)}, f32[2,64,64]{2,1,0:T(8,128)S(1)}, f32[3,1,64]{2,1,0:T(1,128)S(1)}, f32[4,64]{1,0:...) custom-call(f32[3,1,512]{2,1,0:T(1,128)} %bitcast.25, ...), custom_call_target="tpu_custom_call" | custom-call | flops 500000000 | bytes 1000000 | tf_op jit(solution)/shard_map/training_step/pallas_call | solution.py:912
  32.6 1.9 %hand_over.1 = (f32[1,512]{1,0:T(1,128)}, f32[4,64]{1,0:T(4,128)}, f32[2,64,64]{2,1,0:T(8,128)}, f32[3,1,64]{2,1,0:T(1,128)}, f32[4,64]{1,0:T(4,128)}, /*index=5...) custom-call(f32[1,512]{1,0:T(1,128)S(1)} %get-tuple-element.33.refs_, ...), custom_call_target="tpu_custom_call" | custom-call | bytes 400000 | tf_op jit(solution)/shard_map/hand_over/pallas_call | solution.py:924

commit v4 on v3

--- a/solution.py
+++ b/solution.py
@@ -745,7 +745,7 @@
     greet(3)
     prepare_backward(0)
     for face in faces:
-        halo(face).wait()
+        halo(face).wait_recv()
     for face in range(6):
         prepare_forward(3 + face, *face_affine(face))
     for k in range(7):
@@ -829,11 +829,8 @@
     every(gather_copies, False, "wait_send")
     for tile in range(TILES):
         pl.when(here != owners[tile])(tile_copy(tile).wait_send)
-    for tile in range(TILES):
-        pl.when(here != owners[tile])(share_arrival(tile).wait_recv)
-    value = summed[...]
-    give(value, global_first_out, global_mid_out, global_last_out)
-    loss_out[...] = value[71:72, 0:1]
+    for face in faces:
+        halo(face).wait_send()
 
     @pl.when(reducer)
     def _():
@@ -842,14 +839,24 @@
         for number in range(plane - 1):
             share_copy(number).wait_send()
 
+    for tile in range(TILES):
+        rows = slice(8 * tile, 8 * tile + 8)
+        pl.when(here != owners[tile])(share_arrival(tile).wait_recv)
+        if tile < TILES - 1:
+            global_mid_out[0, rows, :] = summed[rows, 0:64]
+            global_mid_out[1, rows, :] = summed[rows, 64:128]
+    value = summed[64:72, :]
+    global_first_out[...] = value[0:4, 0:64]
+    global_last_out[...] = value[4:7, 0:64]
+    loss_out[...] = value[7:8, 0:1]
+
 
 def hand_over(*refs):
     number = len(refs) // 2
     ins, outs, sem = refs[:number], refs[number : 2 * number], refs[2 * number]
-    copies = [pltpu.make_async_copy(ins[k], outs[k], sem.at[k]) for k in range(number - 1)]
+    copies = [pltpu.make_async_copy(ins[k], outs[k], sem.at[k]) for k in range(number)]
     for copy in copies:
         copy.start()
-    outs[number - 1][...] = ins[number - 1][...]
     for copy in copies:
         copy.wait()
 
@@ -925,8 +932,8 @@
         hand_over,
         out_shape=outs,
         in_specs=[whole] * 11,
-        out_specs=[outside] * 10 + [whole],
-        scratch_shapes=[dma((10,))],
+        out_specs=[outside] * 11,
+        scratch_shapes=[dma((11,))],
         compiler_params=pltpu.CompilerParams(vmem_limit_bytes=1 << 20),
         cost_estimate=pl.CostEstimate(flops=0, bytes_accessed=400_000, transcendentals=0),
         name="hand_over",

time: 34.7 us -> 34.2 us (0.986)
  Pallas kernels: 33.9 us -> 33.4 us
    pallas_call x1, Pallas kernels: 1.93 us -> 1.43 us  [step(): pl.pallas_call(hand_over, out_shape=outs, in_specs=[whole] * 11, out_spec...]
where the time goes in v4:
time: 34.2 us; the launch traced here: 34 us
  Pallas kernels  33.4 us (98%)
  between operations  0.66 us (2%)
    pallas_call x1, Pallas kernels, step(): pl.pallas_call(functools.partial(kernel, sizes), out_shape=[vmem(value.sh...  31.9 us
    pallas_call x1, Pallas kernels, step(): pl.pallas_call(hand_over, out_shape=outs, in_specs=[whole] * 11, out_spec...  1.43 us

profile of v4, /device:TPU:1, one launch (start us, length us, event | category | flops | bytes accessed | tf_op | source)
XLA Modules:
  0.0 34.0 jit_solution(1681312098252434136)
XLA Ops:
  0.6 31.9 %training_step.1 = (f32[1,512]{1,0:T(1,128)S(1)}, f32[4,64]{1,0:T(4,128)S(1)}, f32[2,64,64]{2,1,0:T(8,128)S(1)}, f32[3,1,64]{2,1,0:T(1,128)S(1)}, f32[4,64]{1,0:...) custom-call(f32[3,1,512]{2,1,0:T(1,128)} %bitcast.25, ...), custom_call_target="tpu_custom_call" | custom-call | flops 500000000 | bytes 1000000 | tf_op jit(solution)/shard_map/training_step/pallas_call | solution.py:919
  32.6 1.4 %hand_over.1 = (f32[1,512]{1,0:T(1,128)}, f32[4,64]{1,0:T(4,128)}, f32[2,64,64]{2,1,0:T(8,128)}, f32[3,1,64]{2,1,0:T(1,128)}, f32[4,64]{1,0:T(4,128)}, /*index=5...) custom-call(f32[1,512]{1,0:T(1,128)S(1)} %get-tuple-element.33.refs_, ...), custom_call_target="tpu_custom_call" | custom-call | bytes 400000 | tf_op jit(solution)/shard_map/hand_over/pallas_call | solution.py:931
